TPU v7x, 32 devices: a whole 2x2x4 slice. The times are simulated.
32 devices in a mesh: row: 16 (over z, y, core), col: 2 (over x).
Axes of the slice: x: 2, y: 2, z: 4, core: 2. Of those that a mesh axis runs over, the one named last changes fastest.
Arguments:
- p_vals: float32 [64, 4, 128, 128], P('row', 'col'), may hold values from -2 to 2
- p_cols: int32 [64, 4], P('row'), may hold values from 0 to 63, as said below
- out_cols: int32 [64, 4], P('row'), may hold values from 0 to 63, as said below
Outputs:
- c_vals: float32 [64, 4, 128, 128], P('row', 'col')
Inputs may be any that keep to these rules, and one draw needn't show every extreme that they name: Block column indices; p_cols[i, s] // 4 equals (i // 4 + s // 2 - t) mod 16 for some t of 0, 1, 2, 3. `out_cols`: each output block column is p_cols[p_cols[i, s], s2] for some slots s and s2.
All inputs are finite; a program needn't handle non-finite values.
Results may differ from a plain program's by a relative error of at most 0.0003.
Values sent between devices are 32-bit elements; how exact they have to be, the bound alone decides.
No kernel may reach another device: no remote copies, remote signals or barrier semaphores. Data moves between devices by JAX's collectives and lax.ppermute only.
A program may use at most 64 MiB of HBM per device.

v0:
```python
import functools

import jax
import jax.numpy as jnp
from jax import lax
from jax.experimental import pallas as pl
from jax.experimental.pallas import tpu as pltpu
from jax.sharding import PartitionSpec as P

WINDOW = 3
SUBLANES = 8
SMEM = pl.BlockSpec(memory_space=pltpu.SMEM)
VMEM = pl.BlockSpec(memory_space=pltpu.VMEM)
PARAMS = pltpu.CompilerParams(vmem_limit_bytes=48 * 2**20)
SOON = pl.CostEstimate(flops=0, bytes_accessed=0, transcendentals=0)


def split(x):
    high = x.astype(jnp.bfloat16)
    return high, (x - high.astype(jnp.float32)).astype(jnp.bfloat16)


def product(left, right):
    left_high, left_low = split(left)
    right_high, right_low = split(right)
    return jnp.dot(
        jnp.concatenate([left_high, left_low, left_high], axis=1),
        jnp.concatenate([right_high, right_high, right_low], axis=0),
        preferred_element_type=jnp.float32,
    )


def tail_rows(rows):
    return -(-2 * rows // SUBLANES) * SUBLANES


def by_parity(paired, run):
    if paired:
        parity = lax.rem(lax.axis_index("row"), 2)
        pl.when(parity == 0)(lambda: run(0))
        pl.when(parity == 1)(lambda: run(1))
    else:
        run(None)


def pack(blocks, tables, *ahead):
    tall, block = blocks.shape
    rows, slots = tables[0].shape
    tail = tail_rows(rows)

    def kernel(*refs):
        cols_refs, blocks_ref, (out_ref, sem) = refs[:len(tables)], refs[len(tables)], refs[-2:]
        copy = pltpu.make_async_copy(blocks_ref, out_ref.at[pl.ds(0, tall)], sem)
        copy.start()
        row, column = (lax.broadcasted_iota(jnp.int32, (tail, block), d) for d in (0, 1))
        cols = jnp.zeros((tail, block), jnp.float32)
        for n, ref in enumerate(cols_refs):
            for r in range(rows):
                for s in range(slots):
                    here = (row == n * rows + r) & (column == s)
                    cols = jnp.where(here, ref[r, s], cols)
        out_ref[pl.ds(tall, tail)] = cols
        copy.wait()

    return pl.pallas_call(
        kernel,
        out_shape=jax.ShapeDtypeStruct((tall + tail, block), jnp.float32),
        in_specs=[SMEM] * len(tables) + [VMEM] * (1 + len(ahead)),
        out_specs=VMEM,
        scratch_shapes=[pltpu.SemaphoreType.DMA],
        compiler_params=PARAMS,
        cost_estimate=SOON,
    )(*tables, blocks, *ahead)


def repack(tall, even, odd, *ahead):
    def kernel(*refs):
        out_ref, sems = refs[-2:]

        def run(p):
            copies = [
                pltpu.make_async_copy(refs[2 * p].at[pl.ds(0, tall)], out_ref.at[pl.ds(0, tall)], sems.at[0]),
                pltpu.make_async_copy(refs[2 * p + 1].at[pl.ds(tall, tail)], out_ref.at[pl.ds(tall, tail)], sems.at[1]),
            ]
            for copy in copies:
                copy.start()
            for copy in copies:
                copy.wait()

        by_parity(True, run)

    tail = even[1].shape[0] - tall
    return pl.pallas_call(
        kernel,
        out_shape=jax.ShapeDtypeStruct(even[1].shape, jnp.float32),
        in_specs=[VMEM] * (4 + len(ahead)),
        out_specs=VMEM,
        scratch_shapes=[pltpu.SemaphoreType.DMA((2,))],
        compiler_params=PARAMS,
        cost_estimate=SOON,
    )(*even, *odd, *ahead)


def list_pairs(p_cols, ncol, offsets):
    rows, slots = p_cols.shape
    slots_dev = slots // ncol
    nrow = lax.axis_size("row")
    heads, cap = ncol * len(offsets), rows * slots_dev

    def kernel(p_cols_ref, out_ref):
        row_at, col_at = lax.axis_index("row"), lax.axis_index("col")
        for n in range(heads):
            out_ref[n] = 0

        def one_row(i, carry):
            for s in range(slots):
                half, here = s // slots_dev, s % slots_dev
                ahead = lax.rem(col_at + half, ncol)
                k = p_cols_ref[i, ahead * slots_dev + here]
                group, local = lax.div(k, rows), lax.rem(k, rows)
                steps = lax.rem(row_at + ahead - group + nrow, nrow)

                @pl.when(steps < WINDOW)
                def _():
                    head = half * len(offsets) + ahead - steps + WINDOW - 1
                    long = out_ref[head]
                    out_ref[heads + head * cap + long] = (i * slots_dev + here) * rows + local
                    out_ref[head] = long + 1

            return carry

        lax.fori_loop(0, rows, one_row, 0)

    return pl.pallas_call(
        kernel,
        out_shape=jax.ShapeDtypeStruct((heads * (cap + 1),), jnp.int32),
        in_specs=[SMEM],
        out_specs=SMEM,
        compiler_params=PARAMS,
        cost_estimate=SOON,
    )(p_cols)


def index_tile(source, tall, flops, *ahead):
    def kernel(source_ref, *refs):
        out_ref, sem = refs[-2:]
        copy = pltpu.make_async_copy(source_ref.at[pl.ds(tall, out_ref.shape[0])], out_ref, sem)
        copy.start()
        copy.wait()

    return pl.pallas_call(
        kernel,
        out_shape=jax.ShapeDtypeStruct((source.shape[0] - tall, source.shape[1]), jnp.float32),
        in_specs=[VMEM] * (1 + len(ahead)),
        out_specs=VMEM,
        scratch_shapes=[pltpu.SemaphoreType.DMA],
        compiler_params=PARAMS,
        cost_estimate=pl.CostEstimate(flops=flops, bytes_accessed=0, transcendentals=0),
    )(source, *ahead)


def add_products(pairs, offsets, out_cols, left, entries, total, paired, last=False):
    ncol = len(left)
    outs = out_cols.shape[1] // ncol
    block = left[0][0].shape[1]
    rows = out_cols.shape[0]
    slots_dev = out_cols.shape[1] // ncol
    heads, cap = ncol * len(offsets), rows * slots_dev
    shards, indices = [], [pairs, out_cols.astype(jnp.float32)]

    def number(array, known):
        for n, x in enumerate(known):
            if x is array:
                return n
        known.append(array)
        return len(known) - 1

    left_at = [[number(x, shards) for x in part] for part in left]
    plan = [
        (offsets.index(d), p, number(cols, indices), start, [(number(x, shards), half) for x, half in pieces], lefts)
        for d, p, (cols, start), pieces, lefts in entries
    ]
    has_total = total is not None

    def kernel(*refs):
        index_refs, refs = refs[:len(indices)], refs[len(indices):]
        if last:
            total_ref, out_ref, sums, sem = refs[-4:]
            copy = pltpu.make_async_copy(total_ref, sums, sem)
            copy.start()
            copy.wait()
        else:
            sums = refs[-1]
            sums[...] = refs[-2][...] if has_total else jnp.zeros_like(sums)
        col_at = lax.axis_index("col")

        def tile(n, at):
            return refs[n][pl.ds(pl.multiple_of(at * block, block), block), :]

        def run(p):
            for n, q, source, start, pieces, lefts in plan:
                if q is not None and q != p:
                    continue
                for half in lefts:
                    head = half * len(offsets) + n
                    left_shard = left_at[half][p if len(left_at[half]) > 1 else 0]

                    def one_pair(m, carry):
                        pair = index_refs[0][heads + head * cap + m]
                        here, local = lax.div(pair, rows), lax.rem(pair, rows)
                        i = lax.div(here, slots_dev)
                        wanted = [index_refs[1][i, col_at * outs + o] for o in range(outs)]
                        found = []
                        for shard, piece_half in pieces:
                            for t in range(slots_dev):
                                column = index_refs[source][start + local, lax.rem(col_at + piece_half, ncol) * slots_dev + t]
                                found += [(column == wanted[o], shard, t, o) for o in range(outs)]

                        @pl.when(functools.reduce(jnp.logical_or, [match for match, *_ in found]))
                        def _():
                            for match, shard, t, o in found:

                                @pl.when(match)
                                def _():
                                    sums[i, o] += product(tile(left_shard, here), tile(shard, local * slots_dev + t))

                        return carry

                    lax.fori_loop(0, index_refs[0][head], one_pair, 0)

        by_parity(paired, run)
        if last:
            copy = pltpu.make_async_copy(sums, out_ref, sem)
            copy.start()
            copy.wait()

    operands = shards + ([total] if has_total else [])
    shape = (rows, outs, block, block)
    return pl.pallas_call(
        kernel,
        out_shape=jax.ShapeDtypeStruct(shape, jnp.float32),
        in_specs=[SMEM] * len(indices) + [VMEM] * len(operands),
        out_specs=pl.BlockSpec(memory_space=pltpu.HBM) if last else VMEM,
        scratch_shapes=[pltpu.VMEM(shape, jnp.float32), pltpu.SemaphoreType.DMA] if last else [],
        compiler_params=PARAMS,
        cost_estimate=SOON,
    )(*indices, *operands)


def on_device(p_vals, p_cols, out_cols):
    nrow, ncol = lax.axis_size("row"), lax.axis_size("col")
    rows = p_cols.shape[0]

    def permute(x, source):
        pairs = []
        for r in range(nrow):
            for c in range(ncol):
                if source(r, c) is not None:
                    from_row, from_col = source(r, c)
                    pairs.append((from_row % nrow * ncol + from_col % ncol, r * ncol + c))
        return lax.ppermute(x, ("row", "col"), pairs)

    def after(x, *others):
        return lax.optimization_barrier((x, *others))[0]

    own = p_vals.reshape(-1, p_vals.shape[-1])
    offsets = tuple(range(1 - WINDOW, ncol))
    pairs = list_pairs(p_cols, ncol, offsets)

    if ncol == 2 and nrow % 2 == 0:
        def by_core(from_even, from_odd):
            return lambda r, c: (from_odd if r % 2 else from_even)(r, c)

        def across(r, c):
            return r, c + 1

        def behind(r, c):
            return r - 2, c

        def ahead(r, c):
            return r + 2, c

        def beside(r, c):
            return r ^ 1, c

        both = (0, 1)
        tall = own.shape[0]
        first = permute(own, by_core(across, behind))
        own_cols = p_cols.astype(jnp.float32)
        mate_cols = permute(own_cols, beside)
        beside_own = permute(own, beside)
        packed = pack(own, [own_cols, mate_cols], beside_own)
        second = permute(packed, by_core(behind, across))
        next_first = permute(first, lambda r, c: (r + 1, c))
        third = permute(first, lambda r, c: (r, c + 1) if r % 2 else None)
        outgoing = repack(tall, (second, second), (beside_own, packed))
        fourth = permute(outgoing, by_core(across, ahead))
        left = [[packed], [first, second]]

        def add(entries, total, last=False):
            return add_products(pairs, offsets, out_cols, left, entries, total, True, last)

        back_cols = index_tile(second, tall, 0, outgoing)
        total = add(
            [
                (0, 0, (own_cols, 0), [(packed, 0), (first, 1)], both),
                (0, 1, (own_cols, 0), [(packed, 0), (second, 1)], both),
                (1, 0, (mate_cols, 0), [(beside_own, 0)], both),
                (-1, 1, (mate_cols, 0), [(beside_own, 0)], both),
                (-2, 0, (back_cols, 0), [(second, 0)], both),
            ],
            None,
        )
        beside_other = permute(repack(tall, (first, second), (second, second), total), beside)
        beside_third = permute(third, lambda r, c: None if r % 2 else (r + 1, c))
        late_cols = index_tile(second, tall, 10**9, next_first)
        far_cols = index_tile(fourth, tall, 10**9, late_cols)
        mate_back_cols = index_tile(beside_other, tall, 0, far_cols)
        return add(
            [
                (1, 0, (mate_cols, 0), [(beside_other, 1)], both),
                (-1, 1, (mate_cols, 0), [(beside_other, 1)], both),
                (-2, 0, (late_cols, 0), [(fourth, 1)], both),
                (-2, 1, (mate_back_cols, rows), [(first, 0), (third, 1)], both),
                (-1, 0, (late_cols, rows), [(next_first, 0), (beside_third, 1)], both),
                (1, 1, (far_cols, rows), [(fourth, 0), (next_first, 1)], both),
            ],
            total,
            True,
        )

    left = [[own]] + [[permute(own, lambda r, c, j=j: (r, c + j))] for j in range(1, ncol)]
    halves = tuple(range(ncol))
    own_cols = p_cols.astype(jnp.float32)
    shards, cols = {0: own}, {0: own_cols}
    for d in offsets:
        if d:
            shards[d], cols[d] = (permute(x, lambda r, c, d=d: (r + d, c)) for x in (own, own_cols))
    total = None
    for j in halves:
        layer = {d: permute(x, lambda r, c, j=j: (r, c + j)) if j else x for d, x in shards.items()}
        entries = [(d, None, (cols[d], 0), [(x, j)], halves) for d, x in layer.items()]
        total = add_products(pairs, offsets, out_cols, left, entries, total, False)
    return total


def solution(mesh):
    placed = (P("row", "col", None, None), P("row", None), P("row", None))
    return jax.shard_map(
        on_device,
        mesh=mesh,
        in_specs=placed,
        out_specs=P("row", "col", None, None),
        check_vma=False,
    )
```

profile of v0, /device:TPU:1, one launch (start us, length us, event | category | flops | bytes accessed | tf_op | source)
XLA Modules:
  0.0 33.3 jit_solution(16730713480602656420)
XLA Ops:
  0.0 0.1 collective-permute-start.1
  0.1 2.7 %collective-permute-start.3 = (f32[1024,128]{1,0:T(8,128)}, f32[1024,128]{1,0:T(8,128)S(1)}, u32[]{:S(2)}, u32[]{:S(2)}) collective-permute-start(f32[1024,128]{1,0:T(8,128)} %bitcast.2), channel_id=1, source_target_pairs={{1,0},{0,1},{30,2},{31,3},{5,4},{4,5},{2,6},{3,7},{9,8},{8,9},{6,1... | collective-permute-start | bytes 1572872 | tf_op jit(solution)/shard_map/ppermute | solution.py:261
  2.7 0.7 %convert_element_type.8.refs_0_.refs_2_ = f32[4,4]{1,0:T(4,128)S(1)} convert(s32[4,4]{1,0:T(4,128)} %p_cols_ref.1) | non-fusion elementwise | flops 16 | bytes 128 | tf_op jit(solution)/shard_map/convert_element_type | solution.py:289
  3.4 0.3 collective-permute-start
  3.7 0.9 %collective-permute-done.refs_1_.refs_3_.refs_2_ = f32[4,4]{1,0:T(4,128)S(1)} collective-permute-done((f32[4,4]{1,0:T(4,128)S(1)}, f32[4,4]{1,0:T(4,128)S(1)}, u32[]{:S(2)}, u32[]{:S(2)}) %collective-permute-start) | collective-permute-done | bytes 96 | tf_op jit(solution)/shard_map/ppermute | solution.py:261
  4.6 0.0 collective-permute-done.1.refs_3_.refs_2_.refs_8_
  4.6 0.0 copy-start
  4.6 1.0 %copy-done = f32[4,2,128,128]{3,2,1,0:T(8,128)S(1)} copy-done((f32[4,2,128,128]{3,2,1,0:T(8,128)S(1)}, f32[4,2,128,128]{3,2,1,0:T(8,128)}, u32[]{:S(2)}) %copy-start) | copy-done | bytes 524312
  5.6 0.7 %shard_map.38.refs_3_.refs_5_.refs_6_ = f32[1032,128]{1,0:T(8,128)S(1)} custom-call(f32[4,4]{1,0:T(4,128)S(1)} %convert_element_type.8.refs_0_.refs_2_, f32[4,4]{1,0:T(4,128)S(1)} %collective-permute-done.refs_1_.refs_3_.refs_2_, f32[1024,128]{1,0:T(8,128)S(1)} %bitcast.3, f32[1024,128]{1,0:T(8,128)S(1)} %collective-permute-done.1.refs_3_.refs_2_.refs_8_), custom_call_target="tpu_custom_call" | custom-call | tf_op jit(solution)/shard_map/pallas_call | solution.py:65
  6.3 0.0 copy-start.1
  6.3 1.3 %collective-permute-start.2 = (f32[1032,128]{1,0:T(8,128)S(1)}, f32[1032,128]{1,0:T(8,128)S(1)}, u32[]{:S(2)}, u32[]{:S(2)}) collective-permute-start(f32[1032,128]{1,0:T(8,128)S(1)} %shard_map.38.refs_3_.refs_5_.refs_6_), channel_id=1, source_target_pairs={{28,0},{29,1},{3,2},{2,3},{0,4},{1,5},{7,6},{6,7},{4,8},{5,9},{11,... | collective-permute-start | bytes 1585160 | tf_op jit(solution)/shard_map/ppermute | solution.py:261
  7.6 5.5 %collective-permute-done.3.refs_6_.refs_0_.refs_7_ = f32[1024,128]{1,0:T(8,128)S(1)} collective-permute-done((f32[1024,128]{1,0:T(8,128)}, f32[1024,128]{1,0:T(8,128)S(1)}, u32[]{:S(2)}, u32[]{:S(2)}) %collective-permute-start.3) | collective-permute-done | bytes 524320 | tf_op jit(solution)/shard_map/ppermute | solution.py:261
  13.1 3.2 %collective-permute-start.7 = (f32[1024,128]{1,0:T(8,128)S(1)}, f32[1024,128]{1,0:T(8,128)S(1)}, u32[]{:S(2)}, u32[]{:S(2)}) collective-permute-start(f32[1024,128]{1,0:T(8,128)S(1)} %collective-permute-done.3.refs_6_.refs_0_.refs_7_), channel_id=1, source_target_pairs={{3,2},{2,3},{7,6},{6,7},{11,10},{10,11},{15,14},{14,15},{19,18},{1... | collective-permute-start | bytes 1572872 | tf_op jit(solution)/shard_map/ppermute | solution.py:261
  16.3 0.1 collective-permute-start.4
  16.4 0.0 collective-permute-done.2.source_ref.refs_0_.refs_1_.refs_7_.refs_2_.refs_3_.refs_8_
  16.4 0.1 shard_map.40.refs_0_
  16.5 0.0 copy-start.2
  16.5 3.8 %collective-permute-start.6 = (f32[1032,128]{1,0:T(8,128)S(1)}, f32[1032,128]{1,0:T(8,128)S(1)}, u32[]{:S(2)}, u32[]{:S(2)}) collective-permute-start(f32[1032,128]{1,0:T(8,128)S(1)} %shard_map.40.refs_0_), channel_id=1, source_target_pairs={{1,0},{0,1},{6,2},{7,3},{5,4},{4,5},{10,6},{11,7},{9,8},{8,9},{14,... | collective-permute-start | bytes 1585160 | tf_op jit(solution)/shard_map/ppermute | solution.py:261
  20.3 0.0 copy-done.1
  20.3 1.4 %shard_map.37.refs_0_ = s32[72]{0:T(128)S(1)} custom-call(s32[4,4]{1,0:T(4,128)S(1)} %copy-done.1), custom_call_target="tpu_custom_call" | custom-call | tf_op jit(solution)/shard_map/pallas_call | solution.py:134
  21.7 0.0 copy-done.2
  21.7 1.8 %shard_map.42.refs_4_.refs_14_ = f32[4,2,128,128]{3,2,1,0:T(8,128)S(1)} custom-call(s32[72]{0:T(128)S(1)} %shard_map.37.refs_0_, f32[4,4]{1,0:T(4,128)S(1)} %convert_element_type.7.refs_1_, f32[4,4]{1,0:T(4,128)S(1)} %convert_element_type.8.refs_0_.refs_2_, f32[4,4]{1,0:T(4,128)S(1)} %collective-permute-done.refs_1_.refs_3_.refs_2_, ...), custom_call_target="tpu_custom_call" | custom-call | tf_op jit(solution)/shard_map/pallas_call | solution.py:239
  23.5 0.1 shard_map.43
  23.6 1.0 %collective-permute-start.5 = (f32[1032,128]{1,0:T(8,128)S(1)}, f32[1032,128]{1,0:T(8,128)S(1)}, u32[]{:S(2)}, u32[]{:S(2)}) collective-permute-start(f32[1032,128]{1,0:T(8,128)S(1)} %shard_map.43), channel_id=1, source_target_pairs={{2,0},{3,1},{0,2},{1,3},{6,4},{7,5},{4,6},{5,7},{10,8},{11,9},{8,1... | collective-permute-start | bytes 1585160 | tf_op jit(solution)/shard_map/ppermute | solution.py:261
  24.6 0.0 collective-permute-done.7.refs_11_
  24.6 2.0 %collective-permute-start.8 = (f32[1024,128]{1,0:T(8,128)S(1)}, f32[1024,128]{1,0:T(8,128)S(1)}, u32[]{:S(2)}, u32[]{:S(2)}) collective-permute-start(f32[1024,128]{1,0:T(8,128)S(1)} %collective-permute-done.7.refs_11_), channel_id=1, source_target_pairs={{2,0},{3,1},{6,4},{7,5},{10,8},{11,9},{14,12},{15,13},{18,16},{19,... | collective-permute-start | bytes 1572872 | tf_op jit(solution)/shard_map/ppermute | solution.py:261
  26.6 3.7 %collective-permute-done.4.refs_0_.refs_12_ = f32[1024,128]{1,0:T(8,128)S(1)} collective-permute-done((f32[1024,128]{1,0:T(8,128)S(1)}, f32[1024,128]{1,0:T(8,128)S(1)}, u32[]{:S(2)}, u32[]{:S(2)}) %collective-permute-start.4) | collective-permute-done | bytes 524320 | tf_op jit(solution)/shard_map/ppermute | solution.py:261
  30.3 0.7 %collective-permute-done.6.source_ref.refs_10_ = f32[1032,128]{1,0:T(8,128)S(1)} collective-permute-done((f32[1032,128]{1,0:T(8,128)S(1)}, f32[1032,128]{1,0:T(8,128)S(1)}, u32[]{:S(2)}, u32[]{:S(2)}) %collective-permute-start.6) | collective-permute-done | bytes 528416 | tf_op jit(solution)/shard_map/ppermute | solution.py:261
  31.0 0.0 collective-permute-done.5.source_ref.refs_9_
  31.0 0.0 collective-permute-done.8.refs_13_
  31.0 2.3 %shard_map.46 = f32[4,2,128,128]{3,2,1,0:T(8,128)} custom-call(s32[72]{0:T(128)S(1)} %shard_map.37.refs_0_, f32[4,4]{1,0:T(4,128)S(1)} %convert_element_type.7.refs_1_, f32[4,4]{1,0:T(4,128)S(1)} %collective-permute-done.refs_1_.refs_3_.refs_2_, f32[8,128]{1,0:T(8,128)S(1)} %shard_map.39.refs_0_.refs_3_, f32[8,128]{1,0:T(8,128)S(1)} %shard_map.45.refs_4_, ...), custom_call_target="tpu_custom_call" | custom-call | tf_op jit(solution)/shard_map/pallas_call | solution.py:239
  (5 shorter events, 0.1 us)
Async XLA Ops:
  0.0 4.6 %collective-permute-start.1 = (f32[1024,128]{1,0:T(8,128)}, f32[1024,128]{1,0:T(8,128)S(1)}, u32[]{:S(2)}, u32[]{:S(2)}) collective-permute-start(f32[1024,128]{1,0:T(8,128)} %bitcast.1), channel_id=1, source_target_pairs={{2,0},{3,1},{0,2},{1,3},{6,4},{7,5},{4,6},{5,7},{10,8},{11,9},{8,1... | collective-permute-start | bytes 1572872 | tf_op jit(solution)/shard_map/ppermute | solution.py:261
  0.1 13.1 %collective-permute-start.3 = (f32[1024,128]{1,0:T(8,128)}, f32[1024,128]{1,0:T(8,128)S(1)}, u32[]{:S(2)}, u32[]{:S(2)}) collective-permute-start(f32[1024,128]{1,0:T(8,128)} %bitcast.2), channel_id=1, source_target_pairs={{1,0},{0,1},{30,2},{31,3},{5,4},{4,5},{2,6},{3,7},{9,8},{8,9},{6,1... | collective-permute-start | bytes 1572872 | tf_op jit(solution)/shard_map/ppermute | solution.py:261
  3.4 1.2 %collective-permute-start = (f32[4,4]{1,0:T(4,128)S(1)}, f32[4,4]{1,0:T(4,128)S(1)}, u32[]{:S(2)}, u32[]{:S(2)}) collective-permute-start(f32[4,4]{1,0:T(4,128)S(1)} %convert_element_type.8.refs_0_.refs_2_), channel_id=1, source_target_pairs={{2,0},{3,1},{0,2},{1,3},{6,4},{7,5},{4,6},{5,7},{10,8},{11,9},{8,1... | collective-permute-start | bytes 200 | tf_op jit(solution)/shard_map/ppermute | solution.py:261
  4.6 1.0 %copy-start = (f32[4,2,128,128]{3,2,1,0:T(8,128)S(1)}, f32[4,2,128,128]{3,2,1,0:T(8,128)}, u32[]{:S(2)}) copy-start(f32[4,2,128,128]{3,2,1,0:T(8,128)} %param.3) | copy-start | bytes 1572868
  6.3 14.0 %copy-start.1 = (s32[4,4]{1,0:T(4,128)S(1)}, s32[4,4]{1,0:T(4,128)}, u32[]{:S(2)}) copy-start(s32[4,4]{1,0:T(4,128)} %p_cols_ref.1) | copy-start | bytes 196
  6.3 10.1 %collective-permute-start.2 = (f32[1032,128]{1,0:T(8,128)S(1)}, f32[1032,128]{1,0:T(8,128)S(1)}, u32[]{:S(2)}, u32[]{:S(2)}) collective-permute-start(f32[1032,128]{1,0:T(8,128)S(1)} %shard_map.38.refs_3_.refs_5_.refs_6_), channel_id=1, source_target_pairs={{28,0},{29,1},{3,2},{2,3},{0,4},{1,5},{7,6},{6,7},{4,8},{5,9},{11,... | collective-permute-start | bytes 1585160 | tf_op jit(solution)/shard_map/ppermute | solution.py:261
  13.1 11.5 %collective-permute-start.7 = (f32[1024,128]{1,0:T(8,128)S(1)}, f32[1024,128]{1,0:T(8,128)S(1)}, u32[]{:S(2)}, u32[]{:S(2)}) collective-permute-start(f32[1024,128]{1,0:T(8,128)S(1)} %collective-permute-done.3.refs_6_.refs_0_.refs_7_), channel_id=1, source_target_pairs={{3,2},{2,3},{7,6},{6,7},{11,10},{10,11},{15,14},{14,15},{19,18},{1... | collective-permute-start | bytes 1572872 | tf_op jit(solution)/shard_map/ppermute | solution.py:261
  16.3 13.9 %collective-permute-start.4 = (f32[1024,128]{1,0:T(8,128)S(1)}, f32[1024,128]{1,0:T(8,128)S(1)}, u32[]{:S(2)}, u32[]{:S(2)}) collective-permute-start(f32[1024,128]{1,0:T(8,128)S(1)} %collective-permute-done.3.refs_6_.refs_0_.refs_7_), channel_id=1, source_target_pairs={{2,0},{3,1},{4,2},{5,3},{6,4},{7,5},{8,6},{9,7},{10,8},{11,9},{12,... | collective-permute-start | bytes 1572872 | tf_op jit(solution)/shard_map/ppermute | solution.py:261
  16.5 5.2 %copy-start.2 = (s32[4,4]{1,0:T(4,128)S(1)}, s32[4,4]{1,0:T(4,128)}, u32[]{:S(2)}) copy-start(s32[4,4]{1,0:T(4,128)} %param.5) | copy-start | bytes 196
  16.5 14.5 %collective-permute-start.6 = (f32[1032,128]{1,0:T(8,128)S(1)}, f32[1032,128]{1,0:T(8,128)S(1)}, u32[]{:S(2)}, u32[]{:S(2)}) collective-permute-start(f32[1032,128]{1,0:T(8,128)S(1)} %shard_map.40.refs_0_), channel_id=1, source_target_pairs={{1,0},{0,1},{6,2},{7,3},{5,4},{4,5},{10,6},{11,7},{9,8},{8,9},{14,... | collective-permute-start | bytes 1585160 | tf_op jit(solution)/shard_map/ppermute | solution.py:261
  23.6 7.4 %collective-permute-start.5 = (f32[1032,128]{1,0:T(8,128)S(1)}, f32[1032,128]{1,0:T(8,128)S(1)}, u32[]{:S(2)}, u32[]{:S(2)}) collective-permute-start(f32[1032,128]{1,0:T(8,128)S(1)} %shard_map.43), channel_id=1, source_target_pairs={{2,0},{3,1},{0,2},{1,3},{6,4},{7,5},{4,6},{5,7},{10,8},{11,9},{8,1... | collective-permute-start | bytes 1585160 | tf_op jit(solution)/shard_map/ppermute | solution.py:261
  24.6 6.4 %collective-permute-start.8 = (f32[1024,128]{1,0:T(8,128)S(1)}, f32[1024,128]{1,0:T(8,128)S(1)}, u32[]{:S(2)}, u32[]{:S(2)}) collective-permute-start(f32[1024,128]{1,0:T(8,128)S(1)} %collective-permute-done.7.refs_11_), channel_id=1, source_target_pairs={{2,0},{3,1},{6,4},{7,5},{10,8},{11,9},{14,12},{15,13},{18,16},{19,... | collective-permute-start | bytes 1572872 | tf_op jit(solution)/shard_map/ppermute | solution.py:261
where the time goes:
time: 34 us; the launch traced here: 33.3 us
  starting transfers between devices  14.2 us (42%)
  waiting for transfers between devices  10.8 us (32%)
  Pallas kernels  6.4 us (19%)
  local copies, waits for them, and re-layouts  1.06 us (3%)
  other arithmetic  0.69 us (2%)
    ppermute x9, starting transfers between devices, permute(): return lax.ppermute(x, ('row', 'col'), pairs)  14.2 us
    ppermute x9, waiting for transfers between devices, permute(): return lax.ppermute(x, ('row', 'col'), pairs)  10.8 us
    pallas_call x2, Pallas kernels, add_products(): pl.pallas_call(kernel, out_shape=jax.ShapeDtypeStruct(shape, jnp.float32)...  4.11 us
    pallas_call x1, Pallas kernels, list_pairs(): pl.pallas_call(kernel, out_shape=jax.ShapeDtypeStruct((heads * (cap + 1),...  1.38 us
    unnamed x6, local copies, waits for them, and re-layouts  1.06 us
    convert_element_type x1, other arithmetic, on_device(): own_cols = p_cols.astype(jnp.float32)  0.68 us
  transfers between devices with their start and end apart: 9, of which 4 were waited for; matrix products, arithmetic and copies ran while one was open for 2% of the time, Pallas kernels for 12%

commit v1 on v0

--- a/solution.py
+++ b/solution.py
@@ -8,6 +8,7 @@
 from jax.sharding import PartitionSpec as P
 
 WINDOW = 3
+TOGETHER = 4
 SUBLANES = 8
 SMEM = pl.BlockSpec(memory_space=pltpu.SMEM)
 VMEM = pl.BlockSpec(memory_space=pltpu.VMEM)
@@ -30,10 +31,6 @@
     )
 
 
-def tail_rows(rows):
-    return -(-2 * rows // SUBLANES) * SUBLANES
-
-
 def by_parity(paired, run):
     if paired:
         parity = lax.rem(lax.axis_index("row"), 2)
@@ -46,7 +43,7 @@
 def pack(blocks, tables, *ahead):
     tall, block = blocks.shape
     rows, slots = tables[0].shape
-    tail = tail_rows(rows)
+    tail = SUBLANES
 
     def kernel(*refs):
         cols_refs, blocks_ref, (out_ref, sem) = refs[:len(tables)], refs[len(tables)], refs[-2:]
@@ -57,7 +54,7 @@
         for n, ref in enumerate(cols_refs):
             for r in range(rows):
                 for s in range(slots):
-                    here = (row == n * rows + r) & (column == s)
+                    here = (row == r) & (column == n * slots + s)
                     cols = jnp.where(here, ref[r, s], cols)
         out_ref[pl.ds(tall, tail)] = cols
         copy.wait()
@@ -101,6 +98,62 @@
     )(*even, *odd, *ahead)
 
 
+def stack(tall, even, odd):
+    def kernel(*refs):
+        out_ref, sems = refs[-2:]
+
+        def run(p):
+            copies = [
+                pltpu.make_async_copy(refs[2 * p + n].at[pl.ds(0, tall)], out_ref.at[pl.ds(n * tall, tall)], sems.at[n])
+                for n in range(2)
+            ]
+            for copy in copies:
+                copy.start()
+            for copy in copies:
+                copy.wait()
+
+        by_parity(True, run)
+
+    return pl.pallas_call(
+        kernel,
+        out_shape=jax.ShapeDtypeStruct((2 * tall, even[0].shape[1]), jnp.float32),
+        in_specs=[VMEM] * 4,
+        out_specs=VMEM,
+        scratch_shapes=[pltpu.SemaphoreType.DMA((2,))],
+        compiler_params=PARAMS,
+        cost_estimate=SOON,
+    )(*even, *odd)
+
+
+def beside_each_other(rows, width, *tiles):
+    arrays = [x for pair in tiles for x in pair]
+
+    def kernel(*refs):
+        out_ref = refs[-1]
+
+        def run(p):
+            shape = (SUBLANES, arrays[0].shape[1])
+            column = lax.broadcasted_iota(jnp.int32, shape, 1)
+            result = jnp.zeros(shape, jnp.float32)
+            for n in range(len(tiles)):
+                ref, tall = refs[2 * n + p], arrays[2 * n + p].shape[0] - SUBLANES
+                moved = ref[pl.ds(tall, SUBLANES), :]
+                moved = pltpu.roll(moved, n * width, 1) if n else moved
+                result = jnp.where((column >= n * width) & (column < (n + 1) * width), moved, result)
+            out_ref[...] = result[:out_ref.shape[0], :out_ref.shape[1]]
+
+        by_parity(True, run)
+
+    return pl.pallas_call(
+        kernel,
+        out_shape=jax.ShapeDtypeStruct((rows, len(tiles) * width), jnp.float32),
+        in_specs=[VMEM] * len(arrays),
+        out_specs=VMEM,
+        compiler_params=PARAMS,
+        cost_estimate=SOON,
+    )(*arrays)
+
+
 def list_pairs(p_cols, ncol, offsets):
     rows, slots = p_cols.shape
     slots_dev = slots // ncol
@@ -110,7 +163,7 @@
     def kernel(p_cols_ref, out_ref):
         row_at, col_at = lax.axis_index("row"), lax.axis_index("col")
         for n in range(heads):
-            out_ref[n] = 0
+            out_ref[n, cap] = 0
 
         def one_row(i, carry):
             for s in range(slots):
@@ -123,9 +176,9 @@
                 @pl.when(steps < WINDOW)
                 def _():
                     head = half * len(offsets) + ahead - steps + WINDOW - 1
-                    long = out_ref[head]
-                    out_ref[heads + head * cap + long] = (i * slots_dev + here) * rows + local
-                    out_ref[head] = long + 1
+                    long = out_ref[head, cap]
+                    out_ref[head, long] = (i * slots_dev + here) * rows + local
+                    out_ref[head, cap] = long + 1
 
             return carry
 
@@ -133,7 +186,7 @@
 
     return pl.pallas_call(
         kernel,
-        out_shape=jax.ShapeDtypeStruct((heads * (cap + 1),), jnp.int32),
+        out_shape=jax.ShapeDtypeStruct((heads, cap + 1), jnp.int32),
         in_specs=[SMEM],
         out_specs=SMEM,
         compiler_params=PARAMS,
@@ -159,13 +212,13 @@
     )(source, *ahead)
 
 
-def add_products(pairs, offsets, out_cols, left, entries, total, paired, last=False):
+def add_products(pairs, offsets, out_cols, left, entries, total, paired):
     ncol = len(left)
     outs = out_cols.shape[1] // ncol
     block = left[0][0].shape[1]
     rows = out_cols.shape[0]
     slots_dev = out_cols.shape[1] // ncol
-    heads, cap = ncol * len(offsets), rows * slots_dev
+    cap = rows * slots_dev
     shards, indices = [], [pairs, out_cols.astype(jnp.float32)]
 
     def number(array, known):
@@ -184,14 +237,8 @@
 
     def kernel(*refs):
         index_refs, refs = refs[:len(indices)], refs[len(indices):]
-        if last:
-            total_ref, out_ref, sums, sem = refs[-4:]
-            copy = pltpu.make_async_copy(total_ref, sums, sem)
-            copy.start()
-            copy.wait()
-        else:
-            sums = refs[-1]
-            sums[...] = refs[-2][...] if has_total else jnp.zeros_like(sums)
+        sums = refs[-1]
+        sums[...] = refs[-2][...] if has_total else jnp.zeros_like(sums)
         col_at = lax.axis_index("col")
 
         def tile(n, at):
@@ -206,14 +253,14 @@
                     left_shard = left_at[half][p if len(left_at[half]) > 1 else 0]
 
                     def one_pair(m, carry):
-                        pair = index_refs[0][heads + head * cap + m]
+                        pair = index_refs[0][head, m]
                         here, local = lax.div(pair, rows), lax.rem(pair, rows)
                         i = lax.div(here, slots_dev)
                         wanted = [index_refs[1][i, col_at * outs + o] for o in range(outs)]
                         found = []
                         for shard, piece_half in pieces:
                             for t in range(slots_dev):
-                                column = index_refs[source][start + local, lax.rem(col_at + piece_half, ncol) * slots_dev + t]
+                                column = index_refs[source][local, start + lax.rem(col_at + piece_half, ncol) * slots_dev + t]
                                 found += [(column == wanted[o], shard, t, o) for o in range(outs)]
 
                         @pl.when(functools.reduce(jnp.logical_or, [match for match, *_ in found]))
@@ -226,13 +273,9 @@
 
                         return carry
 
-                    lax.fori_loop(0, index_refs[0][head], one_pair, 0)
+                    lax.fori_loop(0, index_refs[0][head, cap], one_pair, 0)
 
         by_parity(paired, run)
-        if last:
-            copy = pltpu.make_async_copy(sums, out_ref, sem)
-            copy.start()
-            copy.wait()
 
     operands = shards + ([total] if has_total else [])
     shape = (rows, outs, block, block)
@@ -240,11 +283,117 @@
         kernel,
         out_shape=jax.ShapeDtypeStruct(shape, jnp.float32),
         in_specs=[SMEM] * len(indices) + [VMEM] * len(operands),
-        out_specs=pl.BlockSpec(memory_space=pltpu.HBM) if last else VMEM,
-        scratch_shapes=[pltpu.VMEM(shape, jnp.float32), pltpu.SemaphoreType.DMA] if last else [],
+        out_specs=VMEM,
         compiler_params=PARAMS,
         cost_estimate=SOON,
     )(*indices, *operands)
+
+
+def finish(pairs, offsets, tables, wanted_at, left, rights, entries, total):
+    rows, outs, block = total.shape[:3]
+    nright = max(len(part) for part in rights)
+    slots_dev = outs
+    ncol = left.shape[0] // (rows * slots_dev * block)
+    blocks = rows * slots_dev
+    tall = blocks * block
+    cap = blocks
+    targets = rows * outs
+    longest = ncol * blocks * outs * slots_dev * max(sum(len(pieces) for *_, pieces in part) for part in entries)
+    shards, indices = [left], [pairs, tables]
+
+    def number(array, known):
+        for n, x in enumerate(known):
+            if x is array:
+                return n
+        known.append(array)
+        return len(known) - 1
+
+    rights_at = [[number(x, shards) for x in part] for part in rights]
+    plan = [[(offsets.index(d), start, pieces) for d, start, pieces in part] for part in entries]
+
+    def kernel(*refs):
+        brought, refs = refs[:len(indices)], refs[len(indices):]
+        total_ref, out_ref, right, sums, listed, sems, index_sems = refs[len(shards):len(shards) + 7]
+        index_refs = refs[len(shards) + 7:]
+        index_copies = [pltpu.make_async_copy(x, y, index_sems.at[n]) for n, (x, y) in enumerate(zip(brought, index_refs))]
+        for copy in index_copies:
+            copy.start()
+        lefts = refs[0]
+        pairs_ref, tables_ref = index_refs
+        col_at = lax.axis_index("col")
+
+        def run(p):
+            copies = [
+                pltpu.make_async_copy(refs[n].at[pl.ds(0, tall)], right.at[pl.ds(m * tall, tall)], sems.at[m])
+                for m, n in enumerate(rights_at[p])
+            ]
+            copies.append(pltpu.make_async_copy(total_ref, sums.at[pl.ds(0, targets)], sems.at[nright]))
+            for copy in copies:
+                copy.start()
+
+            for copy in index_copies:
+                copy.wait()
+            long = jnp.int32(0)
+            for n, start, pieces in plan[p]:
+                for half in range(ncol):
+                    head = half * len(offsets) + n
+
+                    def one_pair(m, long):
+                        pair = pairs_ref[head, m]
+                        here, local = lax.div(pair, rows), lax.rem(pair, rows)
+                        i = lax.div(here, slots_dev)
+                        for shard, piece_half in pieces:
+                            for t in range(slots_dev):
+                                column = tables_ref[local, start + lax.rem(col_at + piece_half, ncol) * slots_dev + t]
+                                code = (half * blocks + here) * nright * blocks + shard * blocks + local * slots_dev + t
+                                for o in range(outs):
+                                    listed[long] = code * targets + i * outs + o
+                                    long += (column == tables_ref[i, wanted_at + col_at * outs + o]).astype(jnp.int32)
+                        return long
+
+                    long = lax.fori_loop(0, pairs_ref[head, cap], one_pair, long)
+            for copy in copies:
+                copy.wait()
+
+            def tile(ref, at):
+                return ref[pl.ds(pl.multiple_of(at * block, block), block), :]
+
+            def some(m, carry):
+                found = []
+                for n in range(TOGETHER):
+                    at = m * TOGETHER + n
+                    code = listed[jnp.minimum(at, long - 1)]
+                    tiles, target = lax.div(code, targets), lax.rem(code, targets)
+                    result = product(tile(lefts, lax.div(tiles, nright * blocks)), tile(right, lax.rem(tiles, nright * blocks)))
+                    found.append((jnp.where(at < long, target, targets), result))
+                for target, result in found:
+                    sums[target] += result
+                return carry
+
+            lax.fori_loop(0, lax.div(long + TOGETHER - 1, TOGETHER), some, 0)
+
+        by_parity(True, run)
+        copy = pltpu.make_async_copy(sums.at[pl.ds(0, targets)], out_ref, sems.at[0])
+        copy.start()
+        copy.wait()
+
+    result = pl.pallas_call(
+        kernel,
+        out_shape=jax.ShapeDtypeStruct((targets, block, block), jnp.float32),
+        in_specs=[VMEM] * (len(indices) + len(shards) + 1),
+        out_specs=pl.BlockSpec(memory_space=pltpu.HBM),
+        scratch_shapes=[
+            pltpu.VMEM((nright * tall, block), jnp.float32),
+            pltpu.VMEM((targets + 1, block, block), jnp.float32),
+            pltpu.SMEM((longest + 1,), jnp.int32),
+            pltpu.SemaphoreType.DMA((nright + 1,)),
+            pltpu.SemaphoreType.DMA((len(indices),)),
+        ]
+        + [pltpu.SMEM(x.shape, x.dtype) for x in indices],
+        compiler_params=PARAMS,
+        cost_estimate=SOON,
+    )(*indices, *shards, total.reshape(targets, block, block))
+    return result.reshape(total.shape)
 
 
 def on_device(p_vals, p_cols, out_cols):
@@ -267,7 +416,7 @@
     offsets = tuple(range(1 - WINDOW, ncol))
     pairs = list_pairs(p_cols, ncol, offsets)
 
-    if ncol == 2 and nrow % 2 == 0:
+    if ncol == 2 and nrow % 2 == 0 and rows <= SUBLANES and 9 * p_cols.shape[1] <= own.shape[1]:
         def by_core(from_even, from_odd):
             return lambda r, c: (from_odd if r % 2 else from_even)(r, c)
 
@@ -289,7 +438,7 @@
         own_cols = p_cols.astype(jnp.float32)
         mate_cols = permute(own_cols, beside)
         beside_own = permute(own, beside)
-        packed = pack(own, [own_cols, mate_cols], beside_own)
+        packed = pack(own, [own_cols, mate_cols, out_cols.astype(jnp.float32)], beside_own)
         second = permute(packed, by_core(behind, across))
         next_first = permute(first, lambda r, c: (r + 1, c))
         third = permute(first, lambda r, c: (r, c + 1) if r % 2 else None)
@@ -297,11 +446,12 @@
         fourth = permute(outgoing, by_core(across, ahead))
         left = [[packed], [first, second]]
 
-        def add(entries, total, last=False):
-            return add_products(pairs, offsets, out_cols, left, entries, total, True, last)
-
         back_cols = index_tile(second, tall, 0, outgoing)
-        total = add(
+        total = add_products(
+            pairs,
+            offsets,
+            out_cols,
+            left,
             [
                 (0, 0, (own_cols, 0), [(packed, 0), (first, 1)], both),
                 (0, 1, (own_cols, 0), [(packed, 0), (second, 1)], both),
@@ -310,23 +460,35 @@
                 (-2, 0, (back_cols, 0), [(second, 0)], both),
             ],
             None,
+            True,
         )
         beside_other = permute(repack(tall, (first, second), (second, second), total), beside)
         beside_third = permute(third, lambda r, c: None if r % 2 else (r + 1, c))
         late_cols = index_tile(second, tall, 10**9, next_first)
         far_cols = index_tile(fourth, tall, 10**9, late_cols)
-        mate_back_cols = index_tile(beside_other, tall, 0, far_cols)
-        return add(
+        width = 3 * p_cols.shape[1]
+        own_at, mate_at, wanted_at = (n * p_cols.shape[1] for n in range(3))
+        tables = beside_each_other(rows, width, (packed, packed), (late_cols, beside_other), (far_cols, far_cols))
+        return finish(
+            pairs,
+            offsets,
+            tables,
+            wanted_at,
+            stack(tall, (packed, first), (packed, second)),
+            [[beside_other, fourth, next_first, beside_third], [beside_other, first, third, fourth, next_first]],
             [
-                (1, 0, (mate_cols, 0), [(beside_other, 1)], both),
-                (-1, 1, (mate_cols, 0), [(beside_other, 1)], both),
-                (-2, 0, (late_cols, 0), [(fourth, 1)], both),
-                (-2, 1, (mate_back_cols, rows), [(first, 0), (third, 1)], both),
-                (-1, 0, (late_cols, rows), [(next_first, 0), (beside_third, 1)], both),
-                (1, 1, (far_cols, rows), [(fourth, 0), (next_first, 1)], both),
+                [
+                    (1, mate_at, [(0, 1)]),
+                    (-2, width + own_at, [(1, 1)]),
+                    (-1, width + mate_at, [(2, 0), (3, 1)]),
+                ],
+                [
+                    (-1, mate_at, [(0, 1)]),
+                    (-2, width + mate_at, [(1, 0), (2, 1)]),
+                    (1, 2 * width + mate_at, [(3, 0), (4, 1)]),
+                ],
             ],
             total,
-            True,
         )
 
     left = [[own]] + [[permute(own, lambda r, c, j=j: (r, c + j))] for j in range(1, ncol)]

time: 34 us -> 33.4 us (0.982)
  waiting for transfers between devices: 10.8 us -> 9.39 us
  starting transfers between devices: 14.2 us -> 15.5 us
    pallas_call x2 -> x1, Pallas kernels: 4.11 us -> 1.61 us  [add_products(): pl.pallas_call(kernel, out_shape=jax.ShapeDtypeStruct(shape, jnp.float32)...]
    pallas_call x1 -> x4, Pallas kernels: 1.38 us -> 3.68 us  [the longest x1 1.99 us: finish(): pl.pallas_call(kernel, out_shape=jax.ShapeDtypeStruct((targets, block, bl...]
    ppermute x9, waiting for transfers between devices: 10.8 us -> 9.39 us  [permute(): return lax.ppermute(x, ('row', 'col'), pairs)]
    ppermute x9, starting transfers between devices: 14.2 us -> 15.5 us  [permute(): return lax.ppermute(x, ('row', 'col'), pairs)]
  transfers between devices with their start and end apart: 9 -> 9, of which waited for: 4 -> 4; matrix products, arithmetic and copies ran while one was open for 2% -> 2% of each run, Pallas kernels for 12% -> 13%
where the time goes in v1:
time: 33.4 us; the launch traced here: 33 us
  starting transfers between devices  15.5 us (46%)
  waiting for transfers between devices  9.39 us (28%)
  Pallas kernels  6.23 us (19%)
  local copies, waits for them, and re-layouts  1.05 us (3%)
  other arithmetic  0.69 us (2%)
    ppermute x9, starting transfers between devices, permute(): return lax.ppermute(x, ('row', 'col'), pairs)  15.5 us
    ppermute x9, waiting for transfers between devices, permute(): return lax.ppermute(x, ('row', 'col'), pairs)  9.39 us
    pallas_call x1, Pallas kernels, finish(): pl.pallas_call(kernel, out_shape=jax.ShapeDtypeStruct((targets, block, bl...  1.99 us
    pallas_call x1, Pallas kernels, add_products(): pl.pallas_call(kernel, out_shape=jax.ShapeDtypeStruct(shape, jnp.float32)...  1.61 us
    pallas_call x1, Pallas kernels, list_pairs(): pl.pallas_call(kernel, out_shape=jax.ShapeDtypeStruct((heads, cap + 1), j...  1.48 us
    unnamed x6, local copies, waits for them, and re-layouts  1.05 us
    pallas_call x1, Pallas kernels, pack(): pl.pallas_call(kernel, out_shape=jax.ShapeDtypeStruct((tall + tail, block...  0.73 us
    convert_element_type x1, other arithmetic, on_device(): own_cols = p_cols.astype(jnp.float32)  0.68 us
  transfers between devices with their start and end apart: 9, of which 4 were waited for; matrix products, arithmetic and copies ran while one was open for 2% of the time, Pallas kernels for 13%

profile of v1, /device:TPU:1, one launch (start us, length us, event | category | flops | bytes accessed | tf_op | source)
XLA Modules:
  0.0 33.0 jit_solution(16985273642408187030)
XLA Ops:
  0.0 0.0 copy-start.2
  0.0 0.1 collective-permute-start.1
  0.1 2.7 %collective-permute-start.3 = (f32[1024,128]{1,0:T(8,128)}, f32[1024,128]{1,0:T(8,128)S(1)}, u32[]{:S(2)}, u32[]{:S(2)}) collective-permute-start(f32[1024,128]{1,0:T(8,128)} %bitcast.5), channel_id=1, source_target_pairs={{1,0},{0,1},{30,2},{31,3},{5,4},{4,5},{2,6},{3,7},{9,8},{8,9},{6,1... | collective-permute-start | bytes 1572872 | tf_op jit(solution)/shard_map/ppermute | solution.py:410
  2.7 0.7 %convert_element_type.7.refs_0_.refs_2_ = f32[4,4]{1,0:T(4,128)S(1)} convert(s32[4,4]{1,0:T(4,128)} %p_cols_ref.1) | non-fusion elementwise | flops 16 | bytes 128 | tf_op jit(solution)/shard_map/convert_element_type | solution.py:438
  3.4 0.3 collective-permute-start
  3.7 0.0 copy-done.2
  3.7 0.9 %collective-permute-done.refs_1_.refs_3_ = f32[4,4]{1,0:T(4,128)S(1)} collective-permute-done((f32[4,4]{1,0:T(4,128)S(1)}, f32[4,4]{1,0:T(4,128)S(1)}, u32[]{:S(2)}, u32[]{:S(2)}) %collective-permute-start) | collective-permute-done | bytes 96 | tf_op jit(solution)/shard_map/ppermute | solution.py:410
  4.6 0.0 collective-permute-done.1.refs_4_.refs_2_.refs_8_
  4.6 0.0 copy-start
  4.6 1.0 %copy-done = f32[4,2,128,128]{3,2,1,0:T(8,128)S(1)} copy-done((f32[4,2,128,128]{3,2,1,0:T(8,128)S(1)}, f32[4,2,128,128]{3,2,1,0:T(8,128)}, u32[]{:S(2)}) %copy-start) | copy-done | bytes 524312
  5.6 0.7 %shard_map.38.refs_3_.refs_5_.refs_0_.refs_1_.refs_2_ = f32[1032,128]{1,0:T(8,128)S(1)} custom-call(f32[4,4]{1,0:T(4,128)S(1)} %convert_element_type.7.refs_0_.refs_2_, f32[4,4]{1,0:T(4,128)S(1)} %collective-permute-done.refs_1_.refs_3_, f32[4,4]{1,0:T(4,128)S(1)} %convert_element_type.8.refs_2_.refs_1_, f32[1024,128]{1,0:T(8,128)S(1)} %bitcast.6, ...), custom_call_target="tpu_custom_call" | custom-call | tf_op jit(solution)/shard_map/pallas_call | solution.py:62
  6.4 0.0 copy-start.1
  6.4 1.3 %collective-permute-start.2 = (f32[1032,128]{1,0:T(8,128)S(1)}, f32[1032,128]{1,0:T(8,128)S(1)}, u32[]{:S(2)}, u32[]{:S(2)}) collective-permute-start(f32[1032,128]{1,0:T(8,128)S(1)} %shard_map.38.refs_3_.refs_5_.refs_0_.refs_1_.refs_2_), channel_id=1, source_target_pairs={{28,0},{29,1},{3,2},{2,3},{0,4},{1,5},{7,6},{6,7},{4,8},{5,9},{11,... | collective-permute-start | bytes 1585160 | tf_op jit(solution)/shard_map/ppermute | solution.py:410
  7.6 5.4 %collective-permute-done.3.refs_6_.refs_0_.refs_1_.refs_7_ = f32[1024,128]{1,0:T(8,128)S(1)} collective-permute-done((f32[1024,128]{1,0:T(8,128)}, f32[1024,128]{1,0:T(8,128)S(1)}, u32[]{:S(2)}, u32[]{:S(2)}) %collective-permute-start.3) | collective-permute-done | bytes 524320 | tf_op jit(solution)/shard_map/ppermute | solution.py:410
  13.1 3.2 %collective-permute-start.7 = (f32[1024,128]{1,0:T(8,128)S(1)}, f32[1024,128]{1,0:T(8,128)S(1)}, u32[]{:S(2)}, u32[]{:S(2)}) collective-permute-start(f32[1024,128]{1,0:T(8,128)S(1)} %collective-permute-done.3.refs_6_.refs_0_.refs_1_.refs_7_), channel_id=1, source_target_pairs={{3,2},{2,3},{7,6},{6,7},{11,10},{10,11},{15,14},{14,15},{19,18},{1... | collective-permute-start | bytes 1572872 | tf_op jit(solution)/shard_map/ppermute | solution.py:410
  16.3 0.1 collective-permute-start.4
  16.4 0.0 collective-permute-done.2.source_ref.refs_0_.refs_1_.refs_7_.refs_2_.refs_3_
  16.4 0.1 shard_map.40.refs_0_
  16.5 3.9 %collective-permute-start.6 = (f32[1032,128]{1,0:T(8,128)S(1)}, f32[1032,128]{1,0:T(8,128)S(1)}, u32[]{:S(2)}, u32[]{:S(2)}) collective-permute-start(f32[1032,128]{1,0:T(8,128)S(1)} %shard_map.40.refs_0_), channel_id=1, source_target_pairs={{1,0},{0,1},{6,2},{7,3},{5,4},{4,5},{10,6},{11,7},{9,8},{8,9},{14,... | collective-permute-start | bytes 1585160 | tf_op jit(solution)/shard_map/ppermute | solution.py:410
  20.3 0.0 copy-done.1
  20.3 1.5 %shard_map.37.refs_0_ = s32[8,9]{1,0:T(8,128)S(1)} custom-call(s32[4,4]{1,0:T(4,128)S(1)} %copy-done.1), custom_call_target="tpu_custom_call" | custom-call | tf_op jit(solution)/shard_map/pallas_call | solution.py:187
  21.8 1.6 %shard_map.42.refs_4_ = f32[4,2,128,128]{3,2,1,0:T(8,128)S(1)} custom-call(s32[8,9]{1,0:T(8,128)S(1)} %shard_map.37.refs_0_, f32[4,4]{1,0:T(4,128)S(1)} %convert_element_type.8.refs_2_.refs_1_, f32[4,4]{1,0:T(4,128)S(1)} %convert_element_type.7.refs_0_.refs_2_, f32[4,4]{1,0:T(4,128)S(1)} %collective-permute-done.refs_1_.refs_3_, ...), custom_call_target="tpu_custom_call" | custom-call | tf_op jit(solution)/shard_map/pallas_call | solution.py:282
  23.4 0.1 shard_map.43
  23.5 2.1 %collective-permute-start.5 = (f32[1032,128]{1,0:T(8,128)S(1)}, f32[1032,128]{1,0:T(8,128)S(1)}, u32[]{:S(2)}, u32[]{:S(2)}) collective-permute-start(f32[1032,128]{1,0:T(8,128)S(1)} %shard_map.43), channel_id=1, source_target_pairs={{2,0},{3,1},{0,2},{1,3},{6,4},{7,5},{4,6},{5,7},{10,8},{11,9},{8,1... | collective-permute-start | bytes 1585160 | tf_op jit(solution)/shard_map/ppermute | solution.py:410
  25.6 0.0 collective-permute-done.7.refs_8_
  25.6 2.0 %collective-permute-start.8 = (f32[1024,128]{1,0:T(8,128)S(1)}, f32[1024,128]{1,0:T(8,128)S(1)}, u32[]{:S(2)}, u32[]{:S(2)}) collective-permute-start(f32[1024,128]{1,0:T(8,128)S(1)} %collective-permute-done.7.refs_8_), channel_id=1, source_target_pairs={{2,0},{3,1},{6,4},{7,5},{10,8},{11,9},{14,12},{15,13},{18,16},{19,... | collective-permute-start | bytes 1572872 | tf_op jit(solution)/shard_map/ppermute | solution.py:410
  27.6 0.1 shard_map.46.refs_2_
  27.7 2.5 %collective-permute-done.4.refs_0_.refs_5_ = f32[1024,128]{1,0:T(8,128)S(1)} collective-permute-done((f32[1024,128]{1,0:T(8,128)S(1)}, f32[1024,128]{1,0:T(8,128)S(1)}, u32[]{:S(2)}, u32[]{:S(2)}) %collective-permute-start.4) | collective-permute-done | bytes 524320 | tf_op jit(solution)/shard_map/ppermute | solution.py:410
  30.2 0.7 %collective-permute-done.6.source_ref.refs_4_ = f32[1032,128]{1,0:T(8,128)S(1)} collective-permute-done((f32[1032,128]{1,0:T(8,128)S(1)}, f32[1032,128]{1,0:T(8,128)S(1)}, u32[]{:S(2)}, u32[]{:S(2)}) %collective-permute-start.6) | collective-permute-done | bytes 528416 | tf_op jit(solution)/shard_map/ppermute | solution.py:410
  30.9 0.0 collective-permute-done.5.refs_3_
  30.9 0.1 shard_map.45.refs_1_
  31.0 0.0 collective-permute-done.8.refs_6_
  31.0 2.0 %shard_map.47 = f32[8,128,128]{2,1,0:T(8,128)} custom-call(s32[8,9]{1,0:T(8,128)S(1)} %shard_map.37.refs_0_, f32[4,36]{1,0:T(4,128)S(1)} %shard_map.45.refs_1_, f32[2048,128]{1,0:T(8,128)S(1)} %shard_map.46.refs_2_, f32[1032,128]{1,0:T(8,128)S(1)} %collective-permute-done.5.refs_3_, f32[1032,128]{1,0:T(8,128)S(1)} %collective-permute-done.6.source_ref.refs_4_, ...), custom_call_target="tpu_custom_call" | custom-call | tf_op jit(solution)/shard_map/pallas_call | solution.py:380
  (4 shorter events, 0.0 us)
Async XLA Ops:
  0.0 3.7 %copy-start.2 = (s32[4,4]{1,0:T(4,128)S(1)}, s32[4,4]{1,0:T(4,128)}, u32[]{:S(2)}) copy-start(s32[4,4]{1,0:T(4,128)} %param.5) | copy-start | bytes 196
  0.0 4.6 %collective-permute-start.1 = (f32[1024,128]{1,0:T(8,128)}, f32[1024,128]{1,0:T(8,128)S(1)}, u32[]{:S(2)}, u32[]{:S(2)}) collective-permute-start(f32[1024,128]{1,0:T(8,128)} %bitcast.4), channel_id=1, source_target_pairs={{2,0},{3,1},{0,2},{1,3},{6,4},{7,5},{4,6},{5,7},{10,8},{11,9},{8,1... | collective-permute-start | bytes 1572872 | tf_op jit(solution)/shard_map/ppermute | solution.py:410
  0.1 13.0 %collective-permute-start.3 = (f32[1024,128]{1,0:T(8,128)}, f32[1024,128]{1,0:T(8,128)S(1)}, u32[]{:S(2)}, u32[]{:S(2)}) collective-permute-start(f32[1024,128]{1,0:T(8,128)} %bitcast.5), channel_id=1, source_target_pairs={{1,0},{0,1},{30,2},{31,3},{5,4},{4,5},{2,6},{3,7},{9,8},{8,9},{6,1... | collective-permute-start | bytes 1572872 | tf_op jit(solution)/shard_map/ppermute | solution.py:410
  3.4 1.2 %collective-permute-start = (f32[4,4]{1,0:T(4,128)S(1)}, f32[4,4]{1,0:T(4,128)S(1)}, u32[]{:S(2)}, u32[]{:S(2)}) collective-permute-start(f32[4,4]{1,0:T(4,128)S(1)} %convert_element_type.7.refs_0_.refs_2_), channel_id=1, source_target_pairs={{2,0},{3,1},{0,2},{1,3},{6,4},{7,5},{4,6},{5,7},{10,8},{11,9},{8,1... | collective-permute-start | bytes 200 | tf_op jit(solution)/shard_map/ppermute | solution.py:410
  4.6 1.0 %copy-start = (f32[4,2,128,128]{3,2,1,0:T(8,128)S(1)}, f32[4,2,128,128]{3,2,1,0:T(8,128)}, u32[]{:S(2)}) copy-start(f32[4,2,128,128]{3,2,1,0:T(8,128)} %param.3) | copy-start | bytes 1572868
  6.4 13.9 %copy-start.1 = (s32[4,4]{1,0:T(4,128)S(1)}, s32[4,4]{1,0:T(4,128)}, u32[]{:S(2)}) copy-start(s32[4,4]{1,0:T(4,128)} %p_cols_ref.1) | copy-start | bytes 196
  6.4 10.0 %collective-permute-start.2 = (f32[1032,128]{1,0:T(8,128)S(1)}, f32[1032,128]{1,0:T(8,128)S(1)}, u32[]{:S(2)}, u32[]{:S(2)}) collective-permute-start(f32[1032,128]{1,0:T(8,128)S(1)} %shard_map.38.refs_3_.refs_5_.refs_0_.refs_1_.refs_2_), channel_id=1, source_target_pairs={{28,0},{29,1},{3,2},{2,3},{0,4},{1,5},{7,6},{6,7},{4,8},{5,9},{11,... | collective-permute-start | bytes 1585160 | tf_op jit(solution)/shard_map/ppermute | solution.py:410
  13.1 12.6 %collective-permute-start.7 = (f32[1024,128]{1,0:T(8,128)S(1)}, f32[1024,128]{1,0:T(8,128)S(1)}, u32[]{:S(2)}, u32[]{:S(2)}) collective-permute-start(f32[1024,128]{1,0:T(8,128)S(1)} %collective-permute-done.3.refs_6_.refs_0_.refs_1_.refs_7_), channel_id=1, source_target_pairs={{3,2},{2,3},{7,6},{6,7},{11,10},{10,11},{15,14},{14,15},{19,18},{1... | collective-permute-start | bytes 1572872 | tf_op jit(solution)/shard_map/ppermute | solution.py:410
  16.3 13.9 %collective-permute-start.4 = (f32[1024,128]{1,0:T(8,128)S(1)}, f32[1024,128]{1,0:T(8,128)S(1)}, u32[]{:S(2)}, u32[]{:S(2)}) collective-permute-start(f32[1024,128]{1,0:T(8,128)S(1)} %collective-permute-done.3.refs_6_.refs_0_.refs_1_.refs_7_), channel_id=1, source_target_pairs={{2,0},{3,1},{4,2},{5,3},{6,4},{7,5},{8,6},{9,7},{10,8},{11,9},{12,... | collective-permute-start | bytes 1572872 | tf_op jit(solution)/shard_map/ppermute | solution.py:410
  16.5 14.4 %collective-permute-start.6 = (f32[1032,128]{1,0:T(8,128)S(1)}, f32[1032,128]{1,0:T(8,128)S(1)}, u32[]{:S(2)}, u32[]{:S(2)}) collective-permute-start(f32[1032,128]{1,0:T(8,128)S(1)} %shard_map.40.refs_0_), channel_id=1, source_target_pairs={{1,0},{0,1},{6,2},{7,3},{5,4},{4,5},{10,6},{11,7},{9,8},{8,9},{14,... | collective-permute-start | bytes 1585160 | tf_op jit(solution)/shard_map/ppermute | solution.py:410
  23.5 7.4 %collective-permute-start.5 = (f32[1032,128]{1,0:T(8,128)S(1)}, f32[1032,128]{1,0:T(8,128)S(1)}, u32[]{:S(2)}, u32[]{:S(2)}) collective-permute-start(f32[1032,128]{1,0:T(8,128)S(1)} %shard_map.43), channel_id=1, source_target_pairs={{2,0},{3,1},{0,2},{1,3},{6,4},{7,5},{4,6},{5,7},{10,8},{11,9},{8,1... | collective-permute-start | bytes 1585160 | tf_op jit(solution)/shard_map/ppermute | solution.py:410
  25.6 5.4 %collective-permute-start.8 = (f32[1024,128]{1,0:T(8,128)S(1)}, f32[1024,128]{1,0:T(8,128)S(1)}, u32[]{:S(2)}, u32[]{:S(2)}) collective-permute-start(f32[1024,128]{1,0:T(8,128)S(1)} %collective-permute-done.7.refs_8_), channel_id=1, source_target_pairs={{2,0},{3,1},{6,4},{7,5},{10,8},{11,9},{14,12},{15,13},{18,16},{19,... | collective-permute-start | bytes 1572872 | tf_op jit(solution)/shard_map/ppermute | solution.py:410

commit v2 on v1

--- a/solution.py
+++ b/solution.py
@@ -438,7 +438,7 @@
         own_cols = p_cols.astype(jnp.float32)
         mate_cols = permute(own_cols, beside)
         beside_own = permute(own, beside)
-        packed = pack(own, [own_cols, mate_cols, out_cols.astype(jnp.float32)], beside_own)
+        packed = pack(own, [own_cols, mate_cols, out_cols.astype(jnp.float32)])
         second = permute(packed, by_core(behind, across))
         next_first = permute(first, lambda r, c: (r + 1, c))
         third = permute(first, lambda r, c: (r, c + 1) if r % 2 else None)
@@ -500,7 +500,8 @@
             shards[d], cols[d] = (permute(x, lambda r, c, d=d: (r + d, c)) for x in (own, own_cols))
     total = None
     for j in halves:
-        layer = {d: permute(x, lambda r, c, j=j: (r, c + j)) if j else x for d, x in shards.items()}
+        sources = {d: after(x, total) if j else x for d, x in shards.items()}
+        layer = {d: permute(x, lambda r, c, j=j: (r, c + j)) if j else x for d, x in sources.items()}
         entries = [(d, None, (cols[d], 0), [(x, j)], halves) for d, x in layer.items()]
         total = add_products(pairs, offsets, out_cols, left, entries, total, False)
     return total

time: 33.4 us -> 32.2 us (0.964)
  waiting for transfers between devices: 9.39 us -> 6.69 us
  Pallas kernels: 6.23 us -> 7.62 us
    ppermute x9, waiting for transfers between devices: 9.39 us -> 6.69 us  [permute(): return lax.ppermute(x, ('row', 'col'), pairs)]
    pallas_call x1, Pallas kernels: 1.61 us -> 2.86 us  [add_products(): pl.pallas_call(kernel, out_shape=jax.ShapeDtypeStruct(shape, jnp.float32)...]
    unnamed x6 -> x8, local copies, waits for them, and re-layouts: 1.05 us -> 1.05 us
  transfers between devices with their start and end apart: 9 -> 9, of which waited for: 4 -> 3; matrix products, arithmetic and copies ran while one was open for 2% -> 2% of each run, Pallas kernels for 13% -> 17%
where the time goes in v2:
time: 32.2 us; the launch traced here: 31.8 us
  starting transfers between devices  15.6 us (48%)
  Pallas kernels  7.62 us (24%)
  waiting for transfers between devices  6.69 us (21%)
  local copies, waits for them, and re-layouts  1.05 us (3%)
  other arithmetic  0.69 us (2%)
    ppermute x9, starting transfers between devices, permute(): return lax.ppermute(x, ('row', 'col'), pairs)  15.6 us
    ppermute x9, waiting for transfers between devices, permute(): return lax.ppermute(x, ('row', 'col'), pairs)  6.69 us
    pallas_call x1, Pallas kernels, add_products(): pl.pallas_call(kernel, out_shape=jax.ShapeDtypeStruct(shape, jnp.float32)...  2.86 us
    pallas_call x1, Pallas kernels, finish(): pl.pallas_call(kernel, out_shape=jax.ShapeDtypeStruct((targets, block, bl...  2.13 us
    pallas_call x1, Pallas kernels, list_pairs(): pl.pallas_call(kernel, out_shape=jax.ShapeDtypeStruct((heads, cap + 1), j...  1.48 us
    unnamed x8, local copies, waits for them, and re-layouts  1.05 us
    pallas_call x1, Pallas kernels, pack(): pl.pallas_call(kernel, out_shape=jax.ShapeDtypeStruct((tall + tail, block...  0.73 us
    convert_element_type x1, other arithmetic, on_device(): own_cols = p_cols.astype(jnp.float32)  0.68 us
  transfers between devices with their start and end apart: 9, of which 3 were waited for; matrix products, arithmetic and copies ran while one was open for 2% of the time, Pallas kernels for 17%

profile of v2, /device:TPU:1, one launch (start us, length us, event | category | flops | bytes accessed | tf_op | source)
XLA Modules:
  0.0 31.8 jit_solution(4560409855142765537)
XLA Ops:
  0.0 0.0 copy-start.3
  0.0 2.1 %collective-permute-start.2 = (f32[1024,128]{1,0:T(8,128)}, f32[1024,128]{1,0:T(8,128)S(1)}, u32[]{:S(2)}, u32[]{:S(2)}) collective-permute-start(f32[1024,128]{1,0:T(8,128)} %bitcast.4), channel_id=1, source_target_pairs={{1,0},{0,1},{30,2},{31,3},{5,4},{4,5},{2,6},{3,7},{9,8},{8,9},{6,1... | collective-permute-start | bytes 1572872 | tf_op jit(solution)/shard_map/ppermute | solution.py:410
  2.1 0.7 %convert_element_type.7.refs_0_.refs_2_ = f32[4,4]{1,0:T(4,128)S(1)} convert(s32[4,4]{1,0:T(4,128)} %p_cols_ref.1) | non-fusion elementwise | flops 16 | bytes 128 | tf_op jit(solution)/shard_map/convert_element_type | solution.py:438
  2.8 0.9 %collective-permute-start = (f32[4,4]{1,0:T(4,128)S(1)}, f32[4,4]{1,0:T(4,128)S(1)}, u32[]{:S(2)}, u32[]{:S(2)}) collective-permute-start(f32[4,4]{1,0:T(4,128)S(1)} %convert_element_type.7.refs_0_.refs_2_), channel_id=1, source_target_pairs={{2,0},{3,1},{0,2},{1,3},{6,4},{7,5},{4,6},{5,7},{10,8},{11,9},{8,1... | collective-permute-start | bytes 200 | tf_op jit(solution)/shard_map/ppermute | solution.py:410
  3.7 0.0 copy-done.3
  3.7 0.8 %collective-permute-done.refs_1_.refs_3_ = f32[4,4]{1,0:T(4,128)S(1)} collective-permute-done((f32[4,4]{1,0:T(4,128)S(1)}, f32[4,4]{1,0:T(4,128)S(1)}, u32[]{:S(2)}, u32[]{:S(2)}) %collective-permute-start) | collective-permute-done | bytes 96 | tf_op jit(solution)/shard_map/ppermute | solution.py:410
  4.5 0.0 copy-start
  4.5 1.0 %copy-done = f32[4,2,128,128]{3,2,1,0:T(8,128)S(1)} copy-done((f32[4,2,128,128]{3,2,1,0:T(8,128)S(1)}, f32[4,2,128,128]{3,2,1,0:T(8,128)}, u32[]{:S(2)}) %copy-start) | copy-done | bytes 524312
  5.5 0.0 copy-start.1
  5.5 0.7 %shard_map.38.refs_3_.refs_5_.refs_0_.refs_1_.refs_2_ = f32[1032,128]{1,0:T(8,128)S(1)} custom-call(f32[4,4]{1,0:T(4,128)S(1)} %convert_element_type.7.refs_0_.refs_2_, f32[4,4]{1,0:T(4,128)S(1)} %collective-permute-done.refs_1_.refs_3_, f32[4,4]{1,0:T(4,128)S(1)} %convert_element_type.8.refs_2_.refs_1_, f32[1024,128]{1,0:T(8,128)S(1)} %bitcast.5), custom_call_target="tpu_custom_call" | custom-call | tf_op jit(solution)/shard_map/pallas_call | solution.py:62
  6.3 0.0 copy-start.2
  6.3 0.7 %collective-permute-start.1 = (f32[1032,128]{1,0:T(8,128)S(1)}, f32[1032,128]{1,0:T(8,128)S(1)}, u32[]{:S(2)}, u32[]{:S(2)}) collective-permute-start(f32[1032,128]{1,0:T(8,128)S(1)} %shard_map.38.refs_3_.refs_5_.refs_0_.refs_1_.refs_2_), channel_id=1, source_target_pairs={{28,0},{29,1},{3,2},{2,3},{0,4},{1,5},{7,6},{6,7},{4,8},{5,9},{11,... | collective-permute-start | bytes 1585160 | tf_op jit(solution)/shard_map/ppermute | solution.py:410
  7.0 0.0 copy-done.1
  7.0 1.2 %collective-permute-start.4 = (f32[1024,128]{1,0:T(8,128)S(1)}, f32[1024,128]{1,0:T(8,128)S(1)}, u32[]{:S(2)}, u32[]{:S(2)}) collective-permute-start(f32[1024,128]{1,0:T(8,128)S(1)} %bitcast.6), channel_id=1, source_target_pairs={{2,0},{3,1},{0,2},{1,3},{6,4},{7,5},{4,6},{5,7},{10,8},{11,9},{8,1... | collective-permute-start | bytes 1572872 | tf_op jit(solution)/shard_map/ppermute | solution.py:410
  8.2 3.7 %collective-permute-done.2.refs_6_.refs_0_.refs_1_.refs_7_ = f32[1024,128]{1,0:T(8,128)S(1)} collective-permute-done((f32[1024,128]{1,0:T(8,128)}, f32[1024,128]{1,0:T(8,128)S(1)}, u32[]{:S(2)}, u32[]{:S(2)}) %collective-permute-start.2) | collective-permute-done | bytes 524320 | tf_op jit(solution)/shard_map/ppermute | solution.py:410
  11.9 3.7 %collective-permute-start.7 = (f32[1024,128]{1,0:T(8,128)S(1)}, f32[1024,128]{1,0:T(8,128)S(1)}, u32[]{:S(2)}, u32[]{:S(2)}) collective-permute-start(f32[1024,128]{1,0:T(8,128)S(1)} %collective-permute-done.2.refs_6_.refs_0_.refs_1_.refs_7_), channel_id=1, source_target_pairs={{3,2},{2,3},{7,6},{6,7},{11,10},{10,11},{15,14},{14,15},{19,18},{1... | collective-permute-start | bytes 1572872 | tf_op jit(solution)/shard_map/ppermute | solution.py:410
  15.6 0.1 collective-permute-start.3
  15.7 0.0 collective-permute-done.4.refs_2_.refs_8_
  15.7 0.0 collective-permute-done.1.source_ref.refs_0_.refs_1_.refs_7_.refs_2_.refs_3_
  15.7 0.1 shard_map.40.refs_0_
  15.8 4.5 %collective-permute-start.6 = (f32[1032,128]{1,0:T(8,128)S(1)}, f32[1032,128]{1,0:T(8,128)S(1)}, u32[]{:S(2)}, u32[]{:S(2)}) collective-permute-start(f32[1032,128]{1,0:T(8,128)S(1)} %shard_map.40.refs_0_), channel_id=1, source_target_pairs={{1,0},{0,1},{6,2},{7,3},{5,4},{4,5},{10,6},{11,7},{9,8},{8,9},{14,... | collective-permute-start | bytes 1585160 | tf_op jit(solution)/shard_map/ppermute | solution.py:410
  20.3 0.0 copy-done.2
  20.3 1.5 %shard_map.37.refs_0_ = s32[8,9]{1,0:T(8,128)S(1)} custom-call(s32[4,4]{1,0:T(4,128)S(1)} %copy-done.2), custom_call_target="tpu_custom_call" | custom-call | tf_op jit(solution)/shard_map/pallas_call | solution.py:187
  21.8 2.9 %shard_map.42.refs_4_ = f32[4,2,128,128]{3,2,1,0:T(8,128)S(1)} custom-call(s32[8,9]{1,0:T(8,128)S(1)} %shard_map.37.refs_0_, f32[4,4]{1,0:T(4,128)S(1)} %convert_element_type.8.refs_2_.refs_1_, f32[4,4]{1,0:T(4,128)S(1)} %convert_element_type.7.refs_0_.refs_2_, f32[4,4]{1,0:T(4,128)S(1)} %collective-permute-done.refs_1_.refs_3_, ...), custom_call_target="tpu_custom_call" | custom-call | tf_op jit(solution)/shard_map/pallas_call | solution.py:282
  24.7 0.1 shard_map.43
  24.7 0.1 collective-permute-start.5
  24.8 0.0 collective-permute-done.7.refs_8_
  24.8 2.4 %collective-permute-start.8 = (f32[1024,128]{1,0:T(8,128)S(1)}, f32[1024,128]{1,0:T(8,128)S(1)}, u32[]{:S(2)}, u32[]{:S(2)}) collective-permute-start(f32[1024,128]{1,0:T(8,128)S(1)} %collective-permute-done.7.refs_8_), channel_id=1, source_target_pairs={{2,0},{3,1},{6,4},{7,5},{10,8},{11,9},{14,12},{15,13},{18,16},{19,... | collective-permute-start | bytes 1572872 | tf_op jit(solution)/shard_map/ppermute | solution.py:410
  27.3 0.1 shard_map.46.refs_2_
  27.4 2.2 %collective-permute-done.3.refs_0_.refs_5_ = f32[1024,128]{1,0:T(8,128)S(1)} collective-permute-done((f32[1024,128]{1,0:T(8,128)S(1)}, f32[1024,128]{1,0:T(8,128)S(1)}, u32[]{:S(2)}, u32[]{:S(2)}) %collective-permute-start.3) | collective-permute-done | bytes 524320 | tf_op jit(solution)/shard_map/ppermute | solution.py:410
  29.6 0.0 collective-permute-done.6.source_ref.refs_4_
  29.6 0.0 collective-permute-done.5.refs_3_
  29.6 0.1 shard_map.45.refs_1_
  29.7 0.0 collective-permute-done.8.refs_6_
  29.7 2.1 %shard_map.47 = f32[8,128,128]{2,1,0:T(8,128)} custom-call(s32[8,9]{1,0:T(8,128)S(1)} %shard_map.37.refs_0_, f32[4,36]{1,0:T(4,128)S(1)} %shard_map.45.refs_1_, f32[2048,128]{1,0:T(8,128)S(1)} %shard_map.46.refs_2_, f32[1032,128]{1,0:T(8,128)S(1)} %collective-permute-done.5.refs_3_, f32[1032,128]{1,0:T(8,128)S(1)} %collective-permute-done.6.source_ref.refs_4_, ...), custom_call_target="tpu_custom_call" | custom-call | tf_op jit(solution)/shard_map/pallas_call | solution.py:380
  (4 shorter events, 0.0 us)
Async XLA Ops:
  0.0 3.7 %copy-start.3 = (s32[4,4]{1,0:T(4,128)S(1)}, s32[4,4]{1,0:T(4,128)}, u32[]{:S(2)}) copy-start(s32[4,4]{1,0:T(4,128)} %param.5) | copy-start | bytes 196
  0.0 11.9 %collective-permute-start.2 = (f32[1024,128]{1,0:T(8,128)}, f32[1024,128]{1,0:T(8,128)S(1)}, u32[]{:S(2)}, u32[]{:S(2)}) collective-permute-start(f32[1024,128]{1,0:T(8,128)} %bitcast.4), channel_id=1, source_target_pairs={{1,0},{0,1},{30,2},{31,3},{5,4},{4,5},{2,6},{3,7},{9,8},{8,9},{6,1... | collective-permute-start | bytes 1572872 | tf_op jit(solution)/shard_map/ppermute | solution.py:410
  2.8 1.7 %collective-permute-start = (f32[4,4]{1,0:T(4,128)S(1)}, f32[4,4]{1,0:T(4,128)S(1)}, u32[]{:S(2)}, u32[]{:S(2)}) collective-permute-start(f32[4,4]{1,0:T(4,128)S(1)} %convert_element_type.7.refs_0_.refs_2_), channel_id=1, source_target_pairs={{2,0},{3,1},{0,2},{1,3},{6,4},{7,5},{4,6},{5,7},{10,8},{11,9},{8,1... | collective-permute-start | bytes 200 | tf_op jit(solution)/shard_map/ppermute | solution.py:410
  4.5 1.0 %copy-start = (f32[4,2,128,128]{3,2,1,0:T(8,128)S(1)}, f32[4,2,128,128]{3,2,1,0:T(8,128)}, u32[]{:S(2)}) copy-start(f32[4,2,128,128]{3,2,1,0:T(8,128)} %param.3) | copy-start | bytes 1572868
  5.5 1.4 %copy-start.1 = (f32[4,2,128,128]{3,2,1,0:T(8,128)S(1)}, f32[4,2,128,128]{3,2,1,0:T(8,128)}, u32[]{:S(2)}) copy-start(f32[4,2,128,128]{3,2,1,0:T(8,128)} %param.3) | copy-start | bytes 1572868
  6.3 14.0 %copy-start.2 = (s32[4,4]{1,0:T(4,128)S(1)}, s32[4,4]{1,0:T(4,128)}, u32[]{:S(2)}) copy-start(s32[4,4]{1,0:T(4,128)} %p_cols_ref.1) | copy-start | bytes 196
  6.3 9.4 %collective-permute-start.1 = (f32[1032,128]{1,0:T(8,128)S(1)}, f32[1032,128]{1,0:T(8,128)S(1)}, u32[]{:S(2)}, u32[]{:S(2)}) collective-permute-start(f32[1032,128]{1,0:T(8,128)S(1)} %shard_map.38.refs_3_.refs_5_.refs_0_.refs_1_.refs_2_), channel_id=1, source_target_pairs={{28,0},{29,1},{3,2},{2,3},{0,4},{1,5},{7,6},{6,7},{4,8},{5,9},{11,... | collective-permute-start | bytes 1585160 | tf_op jit(solution)/shard_map/ppermute | solution.py:410
  7.0 8.7 %collective-permute-start.4 = (f32[1024,128]{1,0:T(8,128)S(1)}, f32[1024,128]{1,0:T(8,128)S(1)}, u32[]{:S(2)}, u32[]{:S(2)}) collective-permute-start(f32[1024,128]{1,0:T(8,128)S(1)} %bitcast.6), channel_id=1, source_target_pairs={{2,0},{3,1},{0,2},{1,3},{6,4},{7,5},{4,6},{5,7},{10,8},{11,9},{8,1... | collective-permute-start | bytes 1572872 | tf_op jit(solution)/shard_map/ppermute | solution.py:410
  11.9 12.9 %collective-permute-start.7 = (f32[1024,128]{1,0:T(8,128)S(1)}, f32[1024,128]{1,0:T(8,128)S(1)}, u32[]{:S(2)}, u32[]{:S(2)}) collective-permute-start(f32[1024,128]{1,0:T(8,128)S(1)} %collective-permute-done.2.refs_6_.refs_0_.refs_1_.refs_7_), channel_id=1, source_target_pairs={{3,2},{2,3},{7,6},{6,7},{11,10},{10,11},{15,14},{14,15},{19,18},{1... | collective-permute-start | bytes 1572872 | tf_op jit(solution)/shard_map/ppermute | solution.py:410
  15.6 13.9 %collective-permute-start.3 = (f32[1024,128]{1,0:T(8,128)S(1)}, f32[1024,128]{1,0:T(8,128)S(1)}, u32[]{:S(2)}, u32[]{:S(2)}) collective-permute-start(f32[1024,128]{1,0:T(8,128)S(1)} %collective-permute-done.2.refs_6_.refs_0_.refs_1_.refs_7_), channel_id=1, source_target_pairs={{2,0},{3,1},{4,2},{5,3},{6,4},{7,5},{8,6},{9,7},{10,8},{11,9},{12,... | collective-permute-start | bytes 1572872 | tf_op jit(solution)/shard_map/ppermute | solution.py:410
  15.8 13.8 %collective-permute-start.6 = (f32[1032,128]{1,0:T(8,128)S(1)}, f32[1032,128]{1,0:T(8,128)S(1)}, u32[]{:S(2)}, u32[]{:S(2)}) collective-permute-start(f32[1032,128]{1,0:T(8,128)S(1)} %shard_map.40.refs_0_), channel_id=1, source_target_pairs={{1,0},{0,1},{6,2},{7,3},{5,4},{4,5},{10,6},{11,7},{9,8},{8,9},{14,... | collective-permute-start | bytes 1585160 | tf_op jit(solution)/shard_map/ppermute | solution.py:410
  24.7 4.9 %collective-permute-start.5 = (f32[1032,128]{1,0:T(8,128)S(1)}, f32[1032,128]{1,0:T(8,128)S(1)}, u32[]{:S(2)}, u32[]{:S(2)}) collective-permute-start(f32[1032,128]{1,0:T(8,128)S(1)} %shard_map.43), channel_id=1, source_target_pairs={{2,0},{3,1},{0,2},{1,3},{6,4},{7,5},{4,6},{5,7},{10,8},{11,9},{8,1... | collective-permute-start | bytes 1585160 | tf_op jit(solution)/shard_map/ppermute | solution.py:410
  24.8 4.9 %collective-permute-start.8 = (f32[1024,128]{1,0:T(8,128)S(1)}, f32[1024,128]{1,0:T(8,128)S(1)}, u32[]{:S(2)}, u32[]{:S(2)}) collective-permute-start(f32[1024,128]{1,0:T(8,128)S(1)} %collective-permute-done.7.refs_8_), channel_id=1, source_target_pairs={{2,0},{3,1},{6,4},{7,5},{10,8},{11,9},{14,12},{15,13},{18,16},{19,... | collective-permute-start | bytes 1572872 | tf_op jit(solution)/shard_map/ppermute | solution.py:410

commit v3 on v2

--- a/solution.py
+++ b/solution.py
@@ -438,7 +438,7 @@
         own_cols = p_cols.astype(jnp.float32)
         mate_cols = permute(own_cols, beside)
         beside_own = permute(own, beside)
-        packed = pack(own, [own_cols, mate_cols, out_cols.astype(jnp.float32)])
+        packed = pack(own, [own_cols, mate_cols, out_cols.astype(jnp.float32)], pairs)
         second = permute(packed, by_core(behind, across))
         next_first = permute(first, lambda r, c: (r + 1, c))
         third = permute(first, lambda r, c: (r, c + 1) if r % 2 else None)
@@ -446,28 +446,37 @@
         fourth = permute(outgoing, by_core(across, ahead))
         left = [[packed], [first, second]]
 
+        beside_other = permute(repack(tall, (first, second), (second, second)), beside)
         back_cols = index_tile(second, tall, 0, outgoing)
-        total = add_products(
-            pairs,
-            offsets,
-            out_cols,
-            left,
+        width = 3 * p_cols.shape[1]
+        own_at, mate_at, wanted_at = (n * p_cols.shape[1] for n in range(3))
+
+        def add(entries, total):
+            return add_products(pairs, offsets, out_cols, left, entries, total, True)
+
+        total = add(
             [
                 (0, 0, (own_cols, 0), [(packed, 0), (first, 1)], both),
                 (0, 1, (own_cols, 0), [(packed, 0), (second, 1)], both),
                 (1, 0, (mate_cols, 0), [(beside_own, 0)], both),
                 (-1, 1, (mate_cols, 0), [(beside_own, 0)], both),
-                (-2, 0, (back_cols, 0), [(second, 0)], both),
+                (-2, 0, (back_cols, own_at), [(second, 0)], both),
             ],
             None,
-            True,
         )
-        beside_other = permute(repack(tall, (first, second), (second, second), total), beside)
-        beside_third = permute(third, lambda r, c: None if r % 2 else (r + 1, c))
+        passed_on = repack(tall, (third, packed), (third, packed), total)
+        beside_third = permute(passed_on, lambda r, c: None if r % 2 else (r + 1, c))
+        mate_back_cols = index_tile(beside_other, tall, 0)
+        total = add(
+            [
+                (1, 0, (mate_cols, 0), [(beside_other, 1)], both),
+                (-1, 1, (mate_cols, 0), [(beside_other, 1)], both),
+                (-2, 1, (mate_back_cols, mate_at), [(first, 0)], both),
+            ],
+            total,
+        )
         late_cols = index_tile(second, tall, 10**9, next_first)
-        far_cols = index_tile(fourth, tall, 10**9, late_cols)
-        width = 3 * p_cols.shape[1]
-        own_at, mate_at, wanted_at = (n * p_cols.shape[1] for n in range(3))
+        far_cols = index_tile(fourth, tall, 10**9, late_cols, total)
         tables = beside_each_other(rows, width, (packed, packed), (late_cols, beside_other), (far_cols, far_cols))
         return finish(
             pairs,
@@ -475,17 +484,15 @@
             tables,
             wanted_at,
             stack(tall, (packed, first), (packed, second)),
-            [[beside_other, fourth, next_first, beside_third], [beside_other, first, third, fourth, next_first]],
+            [[fourth, next_first, beside_third], [third, fourth, next_first]],
             [
                 [
-                    (1, mate_at, [(0, 1)]),
-                    (-2, width + own_at, [(1, 1)]),
-                    (-1, width + mate_at, [(2, 0), (3, 1)]),
+                    (-2, width + own_at, [(0, 1)]),
+                    (-1, width + mate_at, [(1, 0), (2, 1)]),
                 ],
                 [
-                    (-1, mate_at, [(0, 1)]),
-                    (-2, width + mate_at, [(1, 0), (2, 1)]),
-                    (1, 2 * width + mate_at, [(3, 0), (4, 1)]),
+                    (-2, width + mate_at, [(0, 1)]),
+                    (1, 2 * width + mate_at, [(1, 0), (2, 1)]),
                 ],
             ],
             total,

time: 32.2 us -> 31.7 us (0.984)
  Pallas kernels: 7.62 us -> 8.79 us
  starting transfers between devices: 15.6 us -> 14.8 us
  waiting for transfers between devices: 6.69 us -> 6.18 us
    pallas_call x1 -> x2, Pallas kernels: 2.86 us -> 4.14 us  [add_products(): pl.pallas_call(kernel, out_shape=jax.ShapeDtypeStruct(shape, jnp.float32)...]
    ppermute x9, starting transfers between devices: 15.6 us -> 14.8 us  [permute(): return lax.ppermute(x, ('row', 'col'), pairs)]
    ppermute x9, waiting for transfers between devices: 6.69 us -> 6.18 us  [permute(): return lax.ppermute(x, ('row', 'col'), pairs)]
  transfers between devices with their start and end apart: 9 -> 9, of which waited for: 3 -> 4; matrix products, arithmetic and copies ran while one was open for 2% -> 2% of each run, Pallas kernels for 17% -> 22%
where the time goes in v3:
time: 31.7 us
  starting transfers between devices  14.8 us (47%)
  Pallas kernels  8.79 us (28%)
  waiting for transfers between devices  6.18 us (19%)
  local copies, waits for them, and re-layouts  1.05 us (3%)
  other arithmetic  0.69 us (2%)
    ppermute x9, starting transfers between devices, permute(): return lax.ppermute(x, ('row', 'col'), pairs)  14.8 us
    ppermute x9, waiting for transfers between devices, permute(): return lax.ppermute(x, ('row', 'col'), pairs)  6.18 us
    pallas_call x2, Pallas kernels, add_products(): pl.pallas_call(kernel, out_shape=jax.ShapeDtypeStruct(shape, jnp.float32)...  4.14 us
    pallas_call x1, Pallas kernels, finish(): pl.pallas_call(kernel, out_shape=jax.ShapeDtypeStruct((targets, block, bl...  1.98 us
    pallas_call x1, Pallas kernels, list_pairs(): pl.pallas_call(kernel, out_shape=jax.ShapeDtypeStruct((heads, cap + 1), j...  1.48 us
    unnamed x8, local copies, waits for them, and re-layouts  1.05 us
    pallas_call x1, Pallas kernels, pack(): pl.pallas_call(kernel, out_shape=jax.ShapeDtypeStruct((tall + tail, block...  0.73 us
    convert_element_type x1, other arithmetic, on_device(): own_cols = p_cols.astype(jnp.float32)  0.68 us
  transfers between devices with their start and end apart: 9, of which 4 were waited for; matrix products, arithmetic and copies ran while one was open for 2% of the time, Pallas kernels for 22%

profile of v3, /device:TPU:1, one launch (start us, length us, event | category | flops | bytes accessed | tf_op | source)
XLA Modules:
  0.0 31.7 jit_solution(3665734154245286841)
XLA Ops:
  0.0 0.0 copy-start.2
  0.0 2.1 %collective-permute-start.2 = (f32[1024,128]{1,0:T(8,128)}, f32[1024,128]{1,0:T(8,128)S(1)}, u32[]{:S(2)}, u32[]{:S(2)}) collective-permute-start(f32[1024,128]{1,0:T(8,128)} %bitcast.4), channel_id=1, source_target_pairs={{1,0},{0,1},{30,2},{31,3},{5,4},{4,5},{2,6},{3,7},{9,8},{8,9},{6,1... | collective-permute-start | bytes 1572872 | tf_op jit(solution)/shard_map/ppermute | solution.py:410
  2.1 0.7 %convert_element_type.8.refs_0_.refs_2_ = f32[4,4]{1,0:T(4,128)S(1)} convert(s32[4,4]{1,0:T(4,128)} %p_cols_ref.1) | non-fusion elementwise | flops 16 | bytes 128 | tf_op jit(solution)/shard_map/convert_element_type | solution.py:438
  2.8 0.0 copy-start.3
  2.8 0.9 %collective-permute-start = (f32[4,4]{1,0:T(4,128)S(1)}, f32[4,4]{1,0:T(4,128)S(1)}, u32[]{:S(2)}, u32[]{:S(2)}) collective-permute-start(f32[4,4]{1,0:T(4,128)S(1)} %convert_element_type.8.refs_0_.refs_2_), channel_id=1, source_target_pairs={{2,0},{3,1},{0,2},{1,3},{6,4},{7,5},{4,6},{5,7},{10,8},{11,9},{8,1... | collective-permute-start | bytes 200 | tf_op jit(solution)/shard_map/ppermute | solution.py:410
  3.7 0.0 copy-done.2
  3.7 1.5 %shard_map.37.refs_4_.refs_0_ = s32[8,9]{1,0:T(8,128)S(1)} custom-call(s32[4,4]{1,0:T(4,128)S(1)} %copy-done.2), custom_call_target="tpu_custom_call" | custom-call | tf_op jit(solution)/shard_map/pallas_call | solution.py:187
  5.2 0.0 copy-done.3
  5.2 0.0 collective-permute-done.refs_1_.refs_3_.refs_2_
  5.2 0.0 copy-start
  5.2 1.0 %copy-done = f32[4,2,128,128]{3,2,1,0:T(8,128)S(1)} copy-done((f32[4,2,128,128]{3,2,1,0:T(8,128)S(1)}, f32[4,2,128,128]{3,2,1,0:T(8,128)}, u32[]{:S(2)}) %copy-start) | copy-done | bytes 524312
  6.3 0.0 copy-start.1
  6.3 0.7 %shard_map.38.refs_3_.refs_5_.refs_4_.refs_0_.refs_1_.refs_2_ = f32[1032,128]{1,0:T(8,128)S(1)} custom-call(f32[4,4]{1,0:T(4,128)S(1)} %convert_element_type.8.refs_0_.refs_2_, f32[4,4]{1,0:T(4,128)S(1)} %collective-permute-done.refs_1_.refs_3_.refs_2_, f32[4,4]{1,0:T(4,128)S(1)} %convert_element_type.9.refs_2_.refs_1_, f32[1024,128]{1,0:T(8,128)S(1)} %bitcast.5, ...), custom_call_target="tpu_custom_call" | custom-call | tf_op jit(solution)/shard_map/pallas_call | solution.py:62
  7.0 0.3 %collective-permute-start.1 = (f32[1032,128]{1,0:T(8,128)S(1)}, f32[1032,128]{1,0:T(8,128)S(1)}, u32[]{:S(2)}, u32[]{:S(2)}) collective-permute-start(f32[1032,128]{1,0:T(8,128)S(1)} %shard_map.38.refs_3_.refs_5_.refs_4_.refs_0_.refs_1_.refs_2_), channel_id=1, source_target_pairs={{28,0},{29,1},{3,2},{2,3},{0,4},{1,5},{7,6},{6,7},{4,8},{5,9},{11,... | collective-permute-start | bytes 1585160 | tf_op jit(solution)/shard_map/ppermute | solution.py:410
  7.3 0.0 copy-done.1
  7.3 1.2 %collective-permute-start.5 = (f32[1024,128]{1,0:T(8,128)S(1)}, f32[1024,128]{1,0:T(8,128)S(1)}, u32[]{:S(2)}, u32[]{:S(2)}) collective-permute-start(f32[1024,128]{1,0:T(8,128)S(1)} %bitcast.6), channel_id=1, source_target_pairs={{2,0},{3,1},{0,2},{1,3},{6,4},{7,5},{4,6},{5,7},{10,8},{11,9},{8,1... | collective-permute-start | bytes 1572872 | tf_op jit(solution)/shard_map/ppermute | solution.py:410
  8.6 3.3 %collective-permute-done.2.refs_0_.refs_6_.refs_5_.refs_1_ = f32[1024,128]{1,0:T(8,128)S(1)} collective-permute-done((f32[1024,128]{1,0:T(8,128)}, f32[1024,128]{1,0:T(8,128)S(1)}, u32[]{:S(2)}, u32[]{:S(2)}) %collective-permute-start.2) | collective-permute-done | bytes 524320 | tf_op jit(solution)/shard_map/ppermute | solution.py:410
  11.9 3.1 %collective-permute-start.7 = (f32[1024,128]{1,0:T(8,128)S(1)}, f32[1024,128]{1,0:T(8,128)S(1)}, u32[]{:S(2)}, u32[]{:S(2)}) collective-permute-start(f32[1024,128]{1,0:T(8,128)S(1)} %collective-permute-done.2.refs_0_.refs_6_.refs_5_.refs_1_), channel_id=1, source_target_pairs={{3,2},{2,3},{7,6},{6,7},{11,10},{10,11},{15,14},{14,15},{19,18},{1... | collective-permute-start | bytes 1572872 | tf_op jit(solution)/shard_map/ppermute | solution.py:410
  15.0 0.1 collective-permute-start.3
  15.1 0.6 %collective-permute-done.1.source_ref.refs_1_.refs_2_.refs_3_.refs_0_.refs_7_.refs_6_ = f32[1032,128]{1,0:T(8,128)S(1)} collective-permute-done((f32[1032,128]{1,0:T(8,128)S(1)}, f32[1032,128]{1,0:T(8,128)S(1)}, u32[]{:S(2)}, u32[]{:S(2)}) %collective-permute-start.1) | collective-permute-done | bytes 528416 | tf_op jit(solution)/shard_map/ppermute | solution.py:410
  15.6 0.1 shard_map.40
  15.7 3.4 %collective-permute-start.4 = (f32[1032,128]{1,0:T(8,128)S(1)}, f32[1032,128]{1,0:T(8,128)S(1)}, u32[]{:S(2)}, u32[]{:S(2)}) collective-permute-start(f32[1032,128]{1,0:T(8,128)S(1)} %shard_map.40), channel_id=1, source_target_pairs={{2,0},{3,1},{0,2},{1,3},{6,4},{7,5},{4,6},{5,7},{10,8},{11,9},{8,1... | collective-permute-start | bytes 1585160 | tf_op jit(solution)/shard_map/ppermute | solution.py:410
  19.1 0.0 collective-permute-done.5.refs_2_.refs_8_
  19.1 0.1 shard_map.41.refs_0_
  19.2 1.6 %collective-permute-start.6 = (f32[1032,128]{1,0:T(8,128)S(1)}, f32[1032,128]{1,0:T(8,128)S(1)}, u32[]{:S(2)}, u32[]{:S(2)}) collective-permute-start(f32[1032,128]{1,0:T(8,128)S(1)} %shard_map.41.refs_0_), channel_id=1, source_target_pairs={{1,0},{0,1},{6,2},{7,3},{5,4},{4,5},{10,6},{11,7},{9,8},{8,9},{14,... | collective-permute-start | bytes 1585160 | tf_op jit(solution)/shard_map/ppermute | solution.py:410
  20.8 2.6 %shard_map.44.refs_8_.refs_4_ = f32[4,2,128,128]{3,2,1,0:T(8,128)S(1)} custom-call(s32[8,9]{1,0:T(8,128)S(1)} %shard_map.37.refs_4_.refs_0_, f32[4,4]{1,0:T(4,128)S(1)} %convert_element_type.9.refs_2_.refs_1_, f32[4,4]{1,0:T(4,128)S(1)} %convert_element_type.8.refs_0_.refs_2_, f32[4,4]{1,0:T(4,128)S(1)} %collective-permute-done.refs_1_.refs_3_.refs_2_, ...), custom_call_target="tpu_custom_call" | custom-call | tf_op jit(solution)/shard_map/pallas_call | solution.py:282
  23.4 0.0 collective-permute-done.7.refs_0_.refs_2_.refs_6_
  23.4 0.1 shard_map.49
  23.5 2.0 %collective-permute-start.8 = (f32[1032,128]{1,0:T(8,128)S(1)}, f32[1032,128]{1,0:T(8,128)S(1)}, u32[]{:S(2)}, u32[]{:S(2)}) collective-permute-start(f32[1032,128]{1,0:T(8,128)S(1)} %shard_map.49), channel_id=1, source_target_pairs={{2,0},{3,1},{6,4},{7,5},{10,8},{11,9},{14,12},{15,13},{18,16},{19,... | collective-permute-start | bytes 1585160 | tf_op jit(solution)/shard_map/ppermute | solution.py:410
  25.5 0.1 shard_map.48.refs_2_
  25.6 0.7 %collective-permute-done.3.refs_0_.refs_4_ = f32[1024,128]{1,0:T(8,128)S(1)} collective-permute-done((f32[1024,128]{1,0:T(8,128)S(1)}, f32[1024,128]{1,0:T(8,128)S(1)}, u32[]{:S(2)}, u32[]{:S(2)}) %collective-permute-start.3) | collective-permute-done | bytes 524320 | tf_op jit(solution)/shard_map/ppermute | solution.py:410
  26.4 0.0 collective-permute-done.4.source_ref.refs_7_.refs_3_
  26.4 1.6 %shard_map.45.refs_1_ = f32[4,2,128,128]{3,2,1,0:T(8,128)S(1)} custom-call(s32[8,9]{1,0:T(8,128)S(1)} %shard_map.37.refs_4_.refs_0_, f32[4,4]{1,0:T(4,128)S(1)} %convert_element_type.9.refs_2_.refs_1_, f32[4,4]{1,0:T(4,128)S(1)} %collective-permute-done.refs_1_.refs_3_.refs_2_, f32[8,128]{1,0:T(8,128)S(1)} %shard_map.42.refs_3_, ...), custom_call_target="tpu_custom_call" | custom-call | tf_op jit(solution)/shard_map/pallas_call | solution.py:282
  28.0 1.6 %collective-permute-done.6.source_ref.refs_3_ = f32[1032,128]{1,0:T(8,128)S(1)} collective-permute-done((f32[1032,128]{1,0:T(8,128)S(1)}, f32[1032,128]{1,0:T(8,128)S(1)}, u32[]{:S(2)}, u32[]{:S(2)}) %collective-permute-start.6) | collective-permute-done | bytes 528416 | tf_op jit(solution)/shard_map/ppermute | solution.py:410
  29.6 0.1 shard_map.47.refs_1_
  29.7 0.0 collective-permute-done.8.refs_5_
  29.7 2.0 %shard_map.50 = f32[8,128,128]{2,1,0:T(8,128)} custom-call(s32[8,9]{1,0:T(8,128)S(1)} %shard_map.37.refs_4_.refs_0_, f32[4,36]{1,0:T(4,128)S(1)} %shard_map.47.refs_1_, f32[2048,128]{1,0:T(8,128)S(1)} %shard_map.48.refs_2_, f32[1032,128]{1,0:T(8,128)S(1)} %collective-permute-done.6.source_ref.refs_3_, ...), custom_call_target="tpu_custom_call" | custom-call | tf_op jit(solution)/shard_map/pallas_call | solution.py:380
  (5 shorter events, 0.1 us)
Async XLA Ops:
  0.0 3.7 %copy-start.2 = (s32[4,4]{1,0:T(4,128)S(1)}, s32[4,4]{1,0:T(4,128)}, u32[]{:S(2)}) copy-start(s32[4,4]{1,0:T(4,128)} %p_cols_ref.1) | copy-start | bytes 196
  0.0 11.9 %collective-permute-start.2 = (f32[1024,128]{1,0:T(8,128)}, f32[1024,128]{1,0:T(8,128)S(1)}, u32[]{:S(2)}, u32[]{:S(2)}) collective-permute-start(f32[1024,128]{1,0:T(8,128)} %bitcast.4), channel_id=1, source_target_pairs={{1,0},{0,1},{30,2},{31,3},{5,4},{4,5},{2,6},{3,7},{9,8},{8,9},{6,1... | collective-permute-start | bytes 1572872 | tf_op jit(solution)/shard_map/ppermute | solution.py:410
  2.8 2.4 %copy-start.3 = (s32[4,4]{1,0:T(4,128)S(1)}, s32[4,4]{1,0:T(4,128)}, u32[]{:S(2)}) copy-start(s32[4,4]{1,0:T(4,128)} %param.5) | copy-start | bytes 196
  2.8 2.4 %collective-permute-start = (f32[4,4]{1,0:T(4,128)S(1)}, f32[4,4]{1,0:T(4,128)S(1)}, u32[]{:S(2)}, u32[]{:S(2)}) collective-permute-start(f32[4,4]{1,0:T(4,128)S(1)} %convert_element_type.8.refs_0_.refs_2_), channel_id=1, source_target_pairs={{2,0},{3,1},{0,2},{1,3},{6,4},{7,5},{4,6},{5,7},{10,8},{11,9},{8,1... | collective-permute-start | bytes 200 | tf_op jit(solution)/shard_map/ppermute | solution.py:410
  5.2 1.0 %copy-start = (f32[4,2,128,128]{3,2,1,0:T(8,128)S(1)}, f32[4,2,128,128]{3,2,1,0:T(8,128)}, u32[]{:S(2)}) copy-start(f32[4,2,128,128]{3,2,1,0:T(8,128)} %param.3) | copy-start | bytes 1572868
  6.3 1.1 %copy-start.1 = (f32[4,2,128,128]{3,2,1,0:T(8,128)S(1)}, f32[4,2,128,128]{3,2,1,0:T(8,128)}, u32[]{:S(2)}) copy-start(f32[4,2,128,128]{3,2,1,0:T(8,128)} %param.3) | copy-start | bytes 1572868
  7.0 8.6 %collective-permute-start.1 = (f32[1032,128]{1,0:T(8,128)S(1)}, f32[1032,128]{1,0:T(8,128)S(1)}, u32[]{:S(2)}, u32[]{:S(2)}) collective-permute-start(f32[1032,128]{1,0:T(8,128)S(1)} %shard_map.38.refs_3_.refs_5_.refs_4_.refs_0_.refs_1_.refs_2_), channel_id=1, source_target_pairs={{28,0},{29,1},{3,2},{2,3},{0,4},{1,5},{7,6},{6,7},{4,8},{5,9},{11,... | collective-permute-start | bytes 1585160 | tf_op jit(solution)/shard_map/ppermute | solution.py:410
  7.3 11.8 %collective-permute-start.5 = (f32[1024,128]{1,0:T(8,128)S(1)}, f32[1024,128]{1,0:T(8,128)S(1)}, u32[]{:S(2)}, u32[]{:S(2)}) collective-permute-start(f32[1024,128]{1,0:T(8,128)S(1)} %bitcast.6), channel_id=1, source_target_pairs={{2,0},{3,1},{0,2},{1,3},{6,4},{7,5},{4,6},{5,7},{10,8},{11,9},{8,1... | collective-permute-start | bytes 1572872 | tf_op jit(solution)/shard_map/ppermute | solution.py:410
  11.9 11.5 %collective-permute-start.7 = (f32[1024,128]{1,0:T(8,128)S(1)}, f32[1024,128]{1,0:T(8,128)S(1)}, u32[]{:S(2)}, u32[]{:S(2)}) collective-permute-start(f32[1024,128]{1,0:T(8,128)S(1)} %collective-permute-done.2.refs_0_.refs_6_.refs_5_.refs_1_), channel_id=1, source_target_pairs={{3,2},{2,3},{7,6},{6,7},{11,10},{10,11},{15,14},{14,15},{19,18},{1... | collective-permute-start | bytes 1572872 | tf_op jit(solution)/shard_map/ppermute | solution.py:410
  15.0 11.4 %collective-permute-start.3 = (f32[1024,128]{1,0:T(8,128)S(1)}, f32[1024,128]{1,0:T(8,128)S(1)}, u32[]{:S(2)}, u32[]{:S(2)}) collective-permute-start(f32[1024,128]{1,0:T(8,128)S(1)} %collective-permute-done.2.refs_0_.refs_6_.refs_5_.refs_1_), channel_id=1, source_target_pairs={{2,0},{3,1},{4,2},{5,3},{6,4},{7,5},{8,6},{9,7},{10,8},{11,9},{12,... | collective-permute-start | bytes 1572872 | tf_op jit(solution)/shard_map/ppermute | solution.py:410
  15.7 10.7 %collective-permute-start.4 = (f32[1032,128]{1,0:T(8,128)S(1)}, f32[1032,128]{1,0:T(8,128)S(1)}, u32[]{:S(2)}, u32[]{:S(2)}) collective-permute-start(f32[1032,128]{1,0:T(8,128)S(1)} %shard_map.40), channel_id=1, source_target_pairs={{2,0},{3,1},{0,2},{1,3},{6,4},{7,5},{4,6},{5,7},{10,8},{11,9},{8,1... | collective-permute-start | bytes 1585160 | tf_op jit(solution)/shard_map/ppermute | solution.py:410
  19.2 10.4 %collective-permute-start.6 = (f32[1032,128]{1,0:T(8,128)S(1)}, f32[1032,128]{1,0:T(8,128)S(1)}, u32[]{:S(2)}, u32[]{:S(2)}) collective-permute-start(f32[1032,128]{1,0:T(8,128)S(1)} %shard_map.41.refs_0_), channel_id=1, source_target_pairs={{1,0},{0,1},{6,2},{7,3},{5,4},{4,5},{10,6},{11,7},{9,8},{8,9},{14,... | collective-permute-start | bytes 1585160 | tf_op jit(solution)/shard_map/ppermute | solution.py:410
  23.5 6.2 %collective-permute-start.8 = (f32[1032,128]{1,0:T(8,128)S(1)}, f32[1032,128]{1,0:T(8,128)S(1)}, u32[]{:S(2)}, u32[]{:S(2)}) collective-permute-start(f32[1032,128]{1,0:T(8,128)S(1)} %shard_map.49), channel_id=1, source_target_pairs={{2,0},{3,1},{6,4},{7,5},{10,8},{11,9},{14,12},{15,13},{18,16},{19,... | collective-permute-start | bytes 1585160 | tf_op jit(solution)/shard_map/ppermute | solution.py:410

commit v4 on v3

--- a/solution.py
+++ b/solution.py
@@ -471,7 +471,8 @@
             [
                 (1, 0, (mate_cols, 0), [(beside_other, 1)], both),
                 (-1, 1, (mate_cols, 0), [(beside_other, 1)], both),
-                (-2, 1, (mate_back_cols, mate_at), [(first, 0)], both),
+                (-2, 1, (mate_back_cols, mate_at), [(first, 0), (third, 1)], both),
+                (-1, 0, (back_cols, mate_at), [(next_first, 0)], both),
             ],
             total,
         )
@@ -484,15 +485,14 @@
             tables,
             wanted_at,
             stack(tall, (packed, first), (packed, second)),
-            [[fourth, next_first, beside_third], [third, fourth, next_first]],
+            [[fourth, beside_third], [fourth, next_first]],
             [
                 [
                     (-2, width + own_at, [(0, 1)]),
-                    (-1, width + mate_at, [(1, 0), (2, 1)]),
+                    (-1, width + mate_at, [(1, 1)]),
                 ],
                 [
-                    (-2, width + mate_at, [(0, 1)]),
-                    (1, 2 * width + mate_at, [(1, 0), (2, 1)]),
+                    (1, 2 * width + mate_at, [(0, 0), (1, 1)]),
                 ],
             ],
             total,

time: 31.7 us -> 31.8 us (level)
  waiting for transfers between devices: 6.18 us -> 6.74 us
  Pallas kernels: 8.79 us -> 8.32 us
    ppermute x9, waiting for transfers between devices: 6.18 us -> 6.74 us  [permute(): return lax.ppermute(x, ('row', 'col'), pairs)]
    pallas_call x2, Pallas kernels: 4.14 us -> 3.66 us  [add_products(): pl.pallas_call(kernel, out_shape=jax.ShapeDtypeStruct(shape, jnp.float32)...]
  transfers between devices with their start and end apart: 9 -> 9, of which waited for: 4 -> 4; matrix products, arithmetic and copies ran while one was open for 2% -> 2% of each run, Pallas kernels for 22% -> 20%
where the time goes in v4:
time: 31.8 us; the launch traced here: 31.7 us
  starting transfers between devices  14.7 us (46%)
  Pallas kernels  8.32 us (26%)
  waiting for transfers between devices  6.74 us (21%)
  local copies, waits for them, and re-layouts  1.05 us (3%)
  other arithmetic  0.69 us (2%)
    ppermute x9, starting transfers between devices, permute(): return lax.ppermute(x, ('row', 'col'), pairs)  14.7 us
    ppermute x9, waiting for transfers between devices, permute(): return lax.ppermute(x, ('row', 'col'), pairs)  6.74 us
    pallas_call x2, Pallas kernels, add_products(): pl.pallas_call(kernel, out_shape=jax.ShapeDtypeStruct(shape, jnp.float32)...  3.66 us
    pallas_call x1, Pallas kernels, finish(): pl.pallas_call(kernel, out_shape=jax.ShapeDtypeStruct((targets, block, bl...  1.99 us
    pallas_call x1, Pallas kernels, list_pairs(): pl.pallas_call(kernel, out_shape=jax.ShapeDtypeStruct((heads, cap + 1), j...  1.48 us
    unnamed x8, local copies, waits for them, and re-layouts  1.05 us
    pallas_call x1, Pallas kernels, pack(): pl.pallas_call(kernel, out_shape=jax.ShapeDtypeStruct((tall + tail, block...  0.73 us
    convert_element_type x1, other arithmetic, on_device(): own_cols = p_cols.astype(jnp.float32)  0.68 us
  transfers between devices with their start and end apart: 9, of which 4 were waited for; matrix products, arithmetic and copies ran while one was open for 2% of the time, Pallas kernels for 20%

profile of v4, /device:TPU:1, one launch (start us, length us, event | category | flops | bytes accessed | tf_op | source)
XLA Modules:
  0.0 31.7 jit_solution(7728095830366956279)
XLA Ops:
  0.0 0.0 copy-start.2
  0.0 2.1 %collective-permute-start.2 = (f32[1024,128]{1,0:T(8,128)}, f32[1024,128]{1,0:T(8,128)S(1)}, u32[]{:S(2)}, u32[]{:S(2)}) collective-permute-start(f32[1024,128]{1,0:T(8,128)} %bitcast.4), channel_id=1, source_target_pairs={{1,0},{0,1},{30,2},{31,3},{5,4},{4,5},{2,6},{3,7},{9,8},{8,9},{6,1... | collective-permute-start | bytes 1572872 | tf_op jit(solution)/shard_map/ppermute | solution.py:410
  2.1 0.7 %convert_element_type.8.refs_0_.refs_2_ = f32[4,4]{1,0:T(4,128)S(1)} convert(s32[4,4]{1,0:T(4,128)} %p_cols_ref.1) | non-fusion elementwise | flops 16 | bytes 128 | tf_op jit(solution)/shard_map/convert_element_type | solution.py:438
  2.8 0.0 copy-start.3
  2.8 0.9 %collective-permute-start = (f32[4,4]{1,0:T(4,128)S(1)}, f32[4,4]{1,0:T(4,128)S(1)}, u32[]{:S(2)}, u32[]{:S(2)}) collective-permute-start(f32[4,4]{1,0:T(4,128)S(1)} %convert_element_type.8.refs_0_.refs_2_), channel_id=1, source_target_pairs={{2,0},{3,1},{0,2},{1,3},{6,4},{7,5},{4,6},{5,7},{10,8},{11,9},{8,1... | collective-permute-start | bytes 200 | tf_op jit(solution)/shard_map/ppermute | solution.py:410
  3.7 0.0 copy-done.2
  3.7 1.5 %shard_map.37.refs_4_.refs_0_ = s32[8,9]{1,0:T(8,128)S(1)} custom-call(s32[4,4]{1,0:T(4,128)S(1)} %copy-done.2), custom_call_target="tpu_custom_call" | custom-call | tf_op jit(solution)/shard_map/pallas_call | solution.py:187
  5.2 0.0 copy-done.3
  5.2 0.0 collective-permute-done.refs_1_.refs_3_.refs_2_
  5.2 0.0 copy-start
  5.2 1.0 %copy-done = f32[4,2,128,128]{3,2,1,0:T(8,128)S(1)} copy-done((f32[4,2,128,128]{3,2,1,0:T(8,128)S(1)}, f32[4,2,128,128]{3,2,1,0:T(8,128)}, u32[]{:S(2)}) %copy-start) | copy-done | bytes 524312
  6.3 0.0 copy-start.1
  6.3 0.7 %shard_map.38.refs_3_.refs_5_.refs_0_.refs_1_.refs_2_ = f32[1032,128]{1,0:T(8,128)S(1)} custom-call(f32[4,4]{1,0:T(4,128)S(1)} %convert_element_type.8.refs_0_.refs_2_, f32[4,4]{1,0:T(4,128)S(1)} %collective-permute-done.refs_1_.refs_3_.refs_2_, f32[4,4]{1,0:T(4,128)S(1)} %convert_element_type.9.refs_2_.refs_1_, f32[1024,128]{1,0:T(8,128)S(1)} %bitcast.5, ...), custom_call_target="tpu_custom_call" | custom-call | tf_op jit(solution)/shard_map/pallas_call | solution.py:62
  7.0 0.3 %collective-permute-start.1 = (f32[1032,128]{1,0:T(8,128)S(1)}, f32[1032,128]{1,0:T(8,128)S(1)}, u32[]{:S(2)}, u32[]{:S(2)}) collective-permute-start(f32[1032,128]{1,0:T(8,128)S(1)} %shard_map.38.refs_3_.refs_5_.refs_0_.refs_1_.refs_2_), channel_id=1, source_target_pairs={{28,0},{29,1},{3,2},{2,3},{0,4},{1,5},{7,6},{6,7},{4,8},{5,9},{11,... | collective-permute-start | bytes 1585160 | tf_op jit(solution)/shard_map/ppermute | solution.py:410
  7.3 0.0 copy-done.1
  7.3 1.2 %collective-permute-start.5 = (f32[1024,128]{1,0:T(8,128)S(1)}, f32[1024,128]{1,0:T(8,128)S(1)}, u32[]{:S(2)}, u32[]{:S(2)}) collective-permute-start(f32[1024,128]{1,0:T(8,128)S(1)} %bitcast.6), channel_id=1, source_target_pairs={{2,0},{3,1},{0,2},{1,3},{6,4},{7,5},{4,6},{5,7},{10,8},{11,9},{8,1... | collective-permute-start | bytes 1572872 | tf_op jit(solution)/shard_map/ppermute | solution.py:410
  8.6 3.3 %collective-permute-done.2.refs_0_.refs_6_.refs_1_ = f32[1024,128]{1,0:T(8,128)S(1)} collective-permute-done((f32[1024,128]{1,0:T(8,128)}, f32[1024,128]{1,0:T(8,128)S(1)}, u32[]{:S(2)}, u32[]{:S(2)}) %collective-permute-start.2) | collective-permute-done | bytes 524320 | tf_op jit(solution)/shard_map/ppermute | solution.py:410
  11.9 3.1 %collective-permute-start.7 = (f32[1024,128]{1,0:T(8,128)S(1)}, f32[1024,128]{1,0:T(8,128)S(1)}, u32[]{:S(2)}, u32[]{:S(2)}) collective-permute-start(f32[1024,128]{1,0:T(8,128)S(1)} %collective-permute-done.2.refs_0_.refs_6_.refs_1_), channel_id=1, source_target_pairs={{3,2},{2,3},{7,6},{6,7},{11,10},{10,11},{15,14},{14,15},{19,18},{1... | collective-permute-start | bytes 1572872 | tf_op jit(solution)/shard_map/ppermute | solution.py:410
  15.0 0.1 collective-permute-start.3
  15.1 0.6 %collective-permute-done.1.source_ref.refs_1_.refs_2_.refs_3_.refs_0_.refs_7_ = f32[1032,128]{1,0:T(8,128)S(1)} collective-permute-done((f32[1032,128]{1,0:T(8,128)S(1)}, f32[1032,128]{1,0:T(8,128)S(1)}, u32[]{:S(2)}, u32[]{:S(2)}) %collective-permute-start.1) | collective-permute-done | bytes 528416 | tf_op jit(solution)/shard_map/ppermute | solution.py:410
  15.6 0.1 shard_map.40
  15.7 3.4 %collective-permute-start.4 = (f32[1032,128]{1,0:T(8,128)S(1)}, f32[1032,128]{1,0:T(8,128)S(1)}, u32[]{:S(2)}, u32[]{:S(2)}) collective-permute-start(f32[1032,128]{1,0:T(8,128)S(1)} %shard_map.40), channel_id=1, source_target_pairs={{2,0},{3,1},{0,2},{1,3},{6,4},{7,5},{4,6},{5,7},{10,8},{11,9},{8,1... | collective-permute-start | bytes 1585160 | tf_op jit(solution)/shard_map/ppermute | solution.py:410
  19.1 0.0 collective-permute-done.5.refs_2_.refs_8_
  19.1 0.1 shard_map.41.refs_0_
  19.2 1.6 %collective-permute-start.6 = (f32[1032,128]{1,0:T(8,128)S(1)}, f32[1032,128]{1,0:T(8,128)S(1)}, u32[]{:S(2)}, u32[]{:S(2)}) collective-permute-start(f32[1032,128]{1,0:T(8,128)S(1)} %shard_map.41.refs_0_), channel_id=1, source_target_pairs={{1,0},{0,1},{6,2},{7,3},{5,4},{4,5},{10,6},{11,7},{9,8},{8,9},{14,... | collective-permute-start | bytes 1585160 | tf_op jit(solution)/shard_map/ppermute | solution.py:410
  20.8 1.6 %shard_map.44.refs_11_.refs_4_ = f32[4,2,128,128]{3,2,1,0:T(8,128)S(1)} custom-call(s32[8,9]{1,0:T(8,128)S(1)} %shard_map.37.refs_4_.refs_0_, f32[4,4]{1,0:T(4,128)S(1)} %convert_element_type.9.refs_2_.refs_1_, f32[4,4]{1,0:T(4,128)S(1)} %convert_element_type.8.refs_0_.refs_2_, f32[4,4]{1,0:T(4,128)S(1)} %collective-permute-done.refs_1_.refs_3_.refs_2_, ...), custom_call_target="tpu_custom_call" | custom-call | tf_op jit(solution)/shard_map/pallas_call | solution.py:282
  22.5 0.0 collective-permute-done.7.refs_9_.refs_0_.refs_2_
  22.5 0.1 shard_map.49
  22.6 1.9 %collective-permute-start.8 = (f32[1032,128]{1,0:T(8,128)S(1)}, f32[1032,128]{1,0:T(8,128)S(1)}, u32[]{:S(2)}, u32[]{:S(2)}) collective-permute-start(f32[1032,128]{1,0:T(8,128)S(1)} %shard_map.49), channel_id=1, source_target_pairs={{2,0},{3,1},{6,4},{7,5},{10,8},{11,9},{14,12},{15,13},{18,16},{19,... | collective-permute-start | bytes 1585160 | tf_op jit(solution)/shard_map/ppermute | solution.py:410
  24.5 0.1 shard_map.48.refs_2_
  24.6 1.8 %collective-permute-done.3.refs_0_.refs_10_.refs_5_ = f32[1024,128]{1,0:T(8,128)S(1)} collective-permute-done((f32[1024,128]{1,0:T(8,128)S(1)}, f32[1024,128]{1,0:T(8,128)S(1)}, u32[]{:S(2)}, u32[]{:S(2)}) %collective-permute-start.3) | collective-permute-done | bytes 524320 | tf_op jit(solution)/shard_map/ppermute | solution.py:410
  26.4 0.0 collective-permute-done.4.source_ref.refs_8_.refs_3_
  26.4 2.0 %shard_map.45.refs_1_ = f32[4,2,128,128]{3,2,1,0:T(8,128)S(1)} custom-call(s32[8,9]{1,0:T(8,128)S(1)} %shard_map.37.refs_4_.refs_0_, f32[4,4]{1,0:T(4,128)S(1)} %convert_element_type.9.refs_2_.refs_1_, f32[4,4]{1,0:T(4,128)S(1)} %collective-permute-done.refs_1_.refs_3_.refs_2_, f32[8,128]{1,0:T(8,128)S(1)} %shard_map.42.refs_3_, ...), custom_call_target="tpu_custom_call" | custom-call | tf_op jit(solution)/shard_map/pallas_call | solution.py:282
  28.5 1.1 %collective-permute-done.6.source_ref.refs_3_ = f32[1032,128]{1,0:T(8,128)S(1)} collective-permute-done((f32[1032,128]{1,0:T(8,128)S(1)}, f32[1032,128]{1,0:T(8,128)S(1)}, u32[]{:S(2)}, u32[]{:S(2)}) %collective-permute-start.6) | collective-permute-done | bytes 528416 | tf_op jit(solution)/shard_map/ppermute | solution.py:410
  29.6 0.1 shard_map.47.refs_1_
  29.7 0.0 collective-permute-done.8.refs_4_
  29.7 2.0 %shard_map.50 = f32[8,128,128]{2,1,0:T(8,128)} custom-call(s32[8,9]{1,0:T(8,128)S(1)} %shard_map.37.refs_4_.refs_0_, f32[4,36]{1,0:T(4,128)S(1)} %shard_map.47.refs_1_, f32[2048,128]{1,0:T(8,128)S(1)} %shard_map.48.refs_2_, f32[1032,128]{1,0:T(8,128)S(1)} %collective-permute-done.6.source_ref.refs_3_, f32[1032,128]{1,0:T(8,128)S(1)} %collective-permute-done.8.refs_4_, ...), custom_call_target="tpu_custom_call" | custom-call | tf_op jit(solution)/shard_map/pallas_call | solution.py:380
  (5 shorter events, 0.1 us)
Async XLA Ops:
  0.0 3.7 %copy-start.2 = (s32[4,4]{1,0:T(4,128)S(1)}, s32[4,4]{1,0:T(4,128)}, u32[]{:S(2)}) copy-start(s32[4,4]{1,0:T(4,128)} %p_cols_ref.1) | copy-start | bytes 196
  0.0 11.9 %collective-permute-start.2 = (f32[1024,128]{1,0:T(8,128)}, f32[1024,128]{1,0:T(8,128)S(1)}, u32[]{:S(2)}, u32[]{:S(2)}) collective-permute-start(f32[1024,128]{1,0:T(8,128)} %bitcast.4), channel_id=1, source_target_pairs={{1,0},{0,1},{30,2},{31,3},{5,4},{4,5},{2,6},{3,7},{9,8},{8,9},{6,1... | collective-permute-start | bytes 1572872 | tf_op jit(solution)/shard_map/ppermute | solution.py:410
  2.8 2.4 %copy-start.3 = (s32[4,4]{1,0:T(4,128)S(1)}, s32[4,4]{1,0:T(4,128)}, u32[]{:S(2)}) copy-start(s32[4,4]{1,0:T(4,128)} %param.5) | copy-start | bytes 196
  2.8 2.4 %collective-permute-start = (f32[4,4]{1,0:T(4,128)S(1)}, f32[4,4]{1,0:T(4,128)S(1)}, u32[]{:S(2)}, u32[]{:S(2)}) collective-permute-start(f32[4,4]{1,0:T(4,128)S(1)} %convert_element_type.8.refs_0_.refs_2_), channel_id=1, source_target_pairs={{2,0},{3,1},{0,2},{1,3},{6,4},{7,5},{4,6},{5,7},{10,8},{11,9},{8,1... | collective-permute-start | bytes 200 | tf_op jit(solution)/shard_map/ppermute | solution.py:410
  5.2 1.0 %copy-start = (f32[4,2,128,128]{3,2,1,0:T(8,128)S(1)}, f32[4,2,128,128]{3,2,1,0:T(8,128)}, u32[]{:S(2)}) copy-start(f32[4,2,128,128]{3,2,1,0:T(8,128)} %param.3) | copy-start | bytes 1572868
  6.3 1.1 %copy-start.1 = (f32[4,2,128,128]{3,2,1,0:T(8,128)S(1)}, f32[4,2,128,128]{3,2,1,0:T(8,128)}, u32[]{:S(2)}) copy-start(f32[4,2,128,128]{3,2,1,0:T(8,128)} %param.3) | copy-start | bytes 1572868
  7.0 8.6 %collective-permute-start.1 = (f32[1032,128]{1,0:T(8,128)S(1)}, f32[1032,128]{1,0:T(8,128)S(1)}, u32[]{:S(2)}, u32[]{:S(2)}) collective-permute-start(f32[1032,128]{1,0:T(8,128)S(1)} %shard_map.38.refs_3_.refs_5_.refs_0_.refs_1_.refs_2_), channel_id=1, source_target_pairs={{28,0},{29,1},{3,2},{2,3},{0,4},{1,5},{7,6},{6,7},{4,8},{5,9},{11,... | collective-permute-start | bytes 1585160 | tf_op jit(solution)/shard_map/ppermute | solution.py:410
  7.3 11.8 %collective-permute-start.5 = (f32[1024,128]{1,0:T(8,128)S(1)}, f32[1024,128]{1,0:T(8,128)S(1)}, u32[]{:S(2)}, u32[]{:S(2)}) collective-permute-start(f32[1024,128]{1,0:T(8,128)S(1)} %bitcast.6), channel_id=1, source_target_pairs={{2,0},{3,1},{0,2},{1,3},{6,4},{7,5},{4,6},{5,7},{10,8},{11,9},{8,1... | collective-permute-start | bytes 1572872 | tf_op jit(solution)/shard_map/ppermute | solution.py:410
  11.9 10.6 %collective-permute-start.7 = (f32[1024,128]{1,0:T(8,128)S(1)}, f32[1024,128]{1,0:T(8,128)S(1)}, u32[]{:S(2)}, u32[]{:S(2)}) collective-permute-start(f32[1024,128]{1,0:T(8,128)S(1)} %collective-permute-done.2.refs_0_.refs_6_.refs_1_), channel_id=1, source_target_pairs={{3,2},{2,3},{7,6},{6,7},{11,10},{10,11},{15,14},{14,15},{19,18},{1... | collective-permute-start | bytes 1572872 | tf_op jit(solution)/shard_map/ppermute | solution.py:410
  15.0 11.4 %collective-permute-start.3 = (f32[1024,128]{1,0:T(8,128)S(1)}, f32[1024,128]{1,0:T(8,128)S(1)}, u32[]{:S(2)}, u32[]{:S(2)}) collective-permute-start(f32[1024,128]{1,0:T(8,128)S(1)} %collective-permute-done.2.refs_0_.refs_6_.refs_1_), channel_id=1, source_target_pairs={{2,0},{3,1},{4,2},{5,3},{6,4},{7,5},{8,6},{9,7},{10,8},{11,9},{12,... | collective-permute-start | bytes 1572872 | tf_op jit(solution)/shard_map/ppermute | solution.py:410
  15.7 10.7 %collective-permute-start.4 = (f32[1032,128]{1,0:T(8,128)S(1)}, f32[1032,128]{1,0:T(8,128)S(1)}, u32[]{:S(2)}, u32[]{:S(2)}) collective-permute-start(f32[1032,128]{1,0:T(8,128)S(1)} %shard_map.40), channel_id=1, source_target_pairs={{2,0},{3,1},{0,2},{1,3},{6,4},{7,5},{4,6},{5,7},{10,8},{11,9},{8,1... | collective-permute-start | bytes 1585160 | tf_op jit(solution)/shard_map/ppermute | solution.py:410
  19.2 10.4 %collective-permute-start.6 = (f32[1032,128]{1,0:T(8,128)S(1)}, f32[1032,128]{1,0:T(8,128)S(1)}, u32[]{:S(2)}, u32[]{:S(2)}) collective-permute-start(f32[1032,128]{1,0:T(8,128)S(1)} %shard_map.41.refs_0_), channel_id=1, source_target_pairs={{1,0},{0,1},{6,2},{7,3},{5,4},{4,5},{10,6},{11,7},{9,8},{8,9},{14,... | collective-permute-start | bytes 1585160 | tf_op jit(solution)/shard_map/ppermute | solution.py:410
  22.6 7.1 %collective-permute-start.8 = (f32[1032,128]{1,0:T(8,128)S(1)}, f32[1032,128]{1,0:T(8,128)S(1)}, u32[]{:S(2)}, u32[]{:S(2)}) collective-permute-start(f32[1032,128]{1,0:T(8,128)S(1)} %shard_map.49), channel_id=1, source_target_pairs={{2,0},{3,1},{6,4},{7,5},{10,8},{11,9},{14,12},{15,13},{18,16},{19,... | collective-permute-start | bytes 1585160 | tf_op jit(solution)/shard_map/ppermute | solution.py:410

commit v5 on v4

--- a/solution.py
+++ b/solution.py
@@ -313,8 +313,8 @@
 
     def kernel(*refs):
         brought, refs = refs[:len(indices)], refs[len(indices):]
-        total_ref, out_ref, right, sums, listed, sems, index_sems = refs[len(shards):len(shards) + 7]
-        index_refs = refs[len(shards) + 7:]
+        total_ref, out_ref, right, sums, listed, touched, sems, index_sems, out_sems = refs[len(shards):len(shards) + 9]
+        index_refs = refs[len(shards) + 9:]
         index_copies = [pltpu.make_async_copy(x, y, index_sems.at[n]) for n, (x, y) in enumerate(zip(brought, index_refs))]
         for copy in index_copies:
             copy.start()
@@ -342,14 +342,22 @@
                         pair = pairs_ref[head, m]
                         here, local = lax.div(pair, rows), lax.rem(pair, rows)
                         i = lax.div(here, slots_dev)
+                        wanted = [tables_ref[i, wanted_at + col_at * outs + o] for o in range(outs)]
+                        found = []
                         for shard, piece_half in pieces:
                             for t in range(slots_dev):
                                 column = tables_ref[local, start + lax.rem(col_at + piece_half, ncol) * slots_dev + t]
-                                code = (half * blocks + here) * nright * blocks + shard * blocks + local * slots_dev + t
-                                for o in range(outs):
-                                    listed[long] = code * targets + i * outs + o
-                                    long += (column == tables_ref[i, wanted_at + col_at * outs + o]).astype(jnp.int32)
-                        return long
+                                found += [(column == wanted[o], shard * blocks + t, o) for o in range(outs)]
+
+                        def append(long):
+                            for match, offset, o in found:
+                                tiles = (half * blocks + here) * nright * blocks + offset + local * slots_dev
+                                listed[long] = tiles * targets + i * outs + o
+                                long += match.astype(jnp.int32)
+                            return long
+
+                        some_match = functools.reduce(jnp.logical_or, [match for match, *_ in found])
+                        return lax.cond(some_match, append, lambda long: long, long)
 
                     long = lax.fori_loop(0, pairs_ref[head, cap], one_pair, long)
             for copy in copies:
@@ -368,14 +376,21 @@
                     found.append((jnp.where(at < long, target, targets), result))
                 for target, result in found:
                     sums[target] += result
+                    touched[target] = 1
                 return carry
 
             lax.fori_loop(0, lax.div(long + TOGETHER - 1, TOGETHER), some, 0)
 
+        early = pltpu.make_async_copy(total_ref, out_ref, sems.at[nright + 1])
+        early.start()
+        for n in range(targets + 1):
+            touched[n] = 0
         by_parity(True, run)
-        copy = pltpu.make_async_copy(sums.at[pl.ds(0, targets)], out_ref, sems.at[0])
-        copy.start()
-        copy.wait()
+        early.wait()
+        for run in ("start", "wait"):
+            for n in range(targets):
+                copy = pltpu.make_async_copy(sums.at[n], out_ref.at[n], out_sems.at[n])
+                pl.when(touched[n] == 1)(getattr(copy, run))
 
     result = pl.pallas_call(
         kernel,
@@ -386,8 +401,10 @@
             pltpu.VMEM((nright * tall, block), jnp.float32),
             pltpu.VMEM((targets + 1, block, block), jnp.float32),
             pltpu.SMEM((longest + 1,), jnp.int32),
-            pltpu.SemaphoreType.DMA((nright + 1,)),
+            pltpu.SMEM((targets + 1,), jnp.int32),
+            pltpu.SemaphoreType.DMA((nright + 2,)),
             pltpu.SemaphoreType.DMA((len(indices),)),
+            pltpu.SemaphoreType.DMA((targets,)),
         ]
         + [pltpu.SMEM(x.shape, x.dtype) for x in indices],
         compiler_params=PARAMS,

time: 31.8 us -> 31.7 us (level)
  starting transfers between devices: 14.7 us -> 14.1 us
  waiting for transfers between devices: 6.74 us -> 7.07 us
    ppermute x9, starting transfers between devices: 14.7 us -> 14.1 us  [permute(): return lax.ppermute(x, ('row', 'col'), pairs)]
    ppermute x9, waiting for transfers between devices: 6.74 us -> 7.07 us  [permute(): return lax.ppermute(x, ('row', 'col'), pairs)]
  transfers between devices with their start and end apart: 9 -> 9, of which waited for: 4 -> 4; matrix products, arithmetic and copies ran while one was open for 2% -> 2% of each run, Pallas kernels for 20% -> 21%
where the time goes in v5:
time: 31.7 us; the launch traced here: 31.4 us
  starting transfers between devices  14.1 us (44%)
  Pallas kernels  8.36 us (26%)
  waiting for transfers between devices  7.07 us (22%)
  local copies, waits for them, and re-layouts  1.05 us (3%)
  other arithmetic  0.69 us (2%)
    ppermute x9, starting transfers between devices, permute(): return lax.ppermute(x, ('row', 'col'), pairs)  14.1 us
    ppermute x9, waiting for transfers between devices, permute(): return lax.ppermute(x, ('row', 'col'), pairs)  7.07 us
    pallas_call x2, Pallas kernels, add_products(): pl.pallas_call(kernel, out_shape=jax.ShapeDtypeStruct(shape, jnp.float32)...  3.92 us
    pallas_call x1, Pallas kernels, finish(): pl.pallas_call(kernel, out_shape=jax.ShapeDtypeStruct((targets, block, bl...  1.77 us
    pallas_call x1, Pallas kernels, list_pairs(): pl.pallas_call(kernel, out_shape=jax.ShapeDtypeStruct((heads, cap + 1), j...  1.48 us
    unnamed x8, local copies, waits for them, and re-layouts  1.05 us
    pallas_call x1, Pallas kernels, pack(): pl.pallas_call(kernel, out_shape=jax.ShapeDtypeStruct((tall + tail, block...  0.73 us
    convert_element_type x1, other arithmetic, on_device(): own_cols = p_cols.astype(jnp.float32)  0.68 us
  transfers between devices with their start and end apart: 9, of which 4 were waited for; matrix products, arithmetic and copies ran while one was open for 2% of the time, Pallas kernels for 21%

profile of v5, /device:TPU:1, one launch (start us, length us, event | category | flops | bytes accessed | tf_op | source)
XLA Modules:
  0.0 31.4 jit_solution(17384890767065422220)
XLA Ops:
  0.0 0.0 copy-start.2
  0.0 2.1 %collective-permute-start.2 = (f32[1024,128]{1,0:T(8,128)}, f32[1024,128]{1,0:T(8,128)S(1)}, u32[]{:S(2)}, u32[]{:S(2)}) collective-permute-start(f32[1024,128]{1,0:T(8,128)} %bitcast.4), channel_id=1, source_target_pairs={{1,0},{0,1},{30,2},{31,3},{5,4},{4,5},{2,6},{3,7},{9,8},{8,9},{6,1... | collective-permute-start | bytes 1572872 | tf_op jit(solution)/shard_map/ppermute | solution.py:427
  2.1 0.7 %convert_element_type.8.refs_0_.refs_2_ = f32[4,4]{1,0:T(4,128)S(1)} convert(s32[4,4]{1,0:T(4,128)} %p_cols_ref.1) | non-fusion elementwise | flops 16 | bytes 128 | tf_op jit(solution)/shard_map/convert_element_type | solution.py:455
  2.8 0.0 copy-start.3
  2.8 0.9 %collective-permute-start = (f32[4,4]{1,0:T(4,128)S(1)}, f32[4,4]{1,0:T(4,128)S(1)}, u32[]{:S(2)}, u32[]{:S(2)}) collective-permute-start(f32[4,4]{1,0:T(4,128)S(1)} %convert_element_type.8.refs_0_.refs_2_), channel_id=1, source_target_pairs={{2,0},{3,1},{0,2},{1,3},{6,4},{7,5},{4,6},{5,7},{10,8},{11,9},{8,1... | collective-permute-start | bytes 200 | tf_op jit(solution)/shard_map/ppermute | solution.py:427
  3.7 0.0 copy-done.2
  3.7 1.5 %shard_map.37.refs_4_.refs_0_ = s32[8,9]{1,0:T(8,128)S(1)} custom-call(s32[4,4]{1,0:T(4,128)S(1)} %copy-done.2), custom_call_target="tpu_custom_call" | custom-call | tf_op jit(solution)/shard_map/pallas_call | solution.py:187
  5.2 0.0 copy-done.3
  5.2 0.0 collective-permute-done.refs_1_.refs_3_.refs_2_
  5.2 0.0 copy-start
  5.2 1.0 %copy-done = f32[4,2,128,128]{3,2,1,0:T(8,128)S(1)} copy-done((f32[4,2,128,128]{3,2,1,0:T(8,128)S(1)}, f32[4,2,128,128]{3,2,1,0:T(8,128)}, u32[]{:S(2)}) %copy-start) | copy-done | bytes 524312
  6.3 0.0 copy-start.1
  6.3 0.7 %shard_map.38.refs_3_.refs_5_.refs_0_.refs_1_.refs_2_ = f32[1032,128]{1,0:T(8,128)S(1)} custom-call(f32[4,4]{1,0:T(4,128)S(1)} %convert_element_type.8.refs_0_.refs_2_, f32[4,4]{1,0:T(4,128)S(1)} %collective-permute-done.refs_1_.refs_3_.refs_2_, f32[4,4]{1,0:T(4,128)S(1)} %convert_element_type.9.refs_2_.refs_1_, f32[1024,128]{1,0:T(8,128)S(1)} %bitcast.5, ...), custom_call_target="tpu_custom_call" | custom-call | tf_op jit(solution)/shard_map/pallas_call | solution.py:62
  7.0 0.3 %collective-permute-start.1 = (f32[1032,128]{1,0:T(8,128)S(1)}, f32[1032,128]{1,0:T(8,128)S(1)}, u32[]{:S(2)}, u32[]{:S(2)}) collective-permute-start(f32[1032,128]{1,0:T(8,128)S(1)} %shard_map.38.refs_3_.refs_5_.refs_0_.refs_1_.refs_2_), channel_id=1, source_target_pairs={{28,0},{29,1},{3,2},{2,3},{0,4},{1,5},{7,6},{6,7},{4,8},{5,9},{11,... | collective-permute-start | bytes 1585160 | tf_op jit(solution)/shard_map/ppermute | solution.py:427
  7.3 0.0 copy-done.1
  7.3 1.2 %collective-permute-start.5 = (f32[1024,128]{1,0:T(8,128)S(1)}, f32[1024,128]{1,0:T(8,128)S(1)}, u32[]{:S(2)}, u32[]{:S(2)}) collective-permute-start(f32[1024,128]{1,0:T(8,128)S(1)} %bitcast.6), channel_id=1, source_target_pairs={{2,0},{3,1},{0,2},{1,3},{6,4},{7,5},{4,6},{5,7},{10,8},{11,9},{8,1... | collective-permute-start | bytes 1572872 | tf_op jit(solution)/shard_map/ppermute | solution.py:427
  8.6 3.3 %collective-permute-done.2.refs_0_.refs_6_.refs_1_ = f32[1024,128]{1,0:T(8,128)S(1)} collective-permute-done((f32[1024,128]{1,0:T(8,128)}, f32[1024,128]{1,0:T(8,128)S(1)}, u32[]{:S(2)}, u32[]{:S(2)}) %collective-permute-start.2) | collective-permute-done | bytes 524320 | tf_op jit(solution)/shard_map/ppermute | solution.py:427
  11.9 3.1 %collective-permute-start.7 = (f32[1024,128]{1,0:T(8,128)S(1)}, f32[1024,128]{1,0:T(8,128)S(1)}, u32[]{:S(2)}, u32[]{:S(2)}) collective-permute-start(f32[1024,128]{1,0:T(8,128)S(1)} %collective-permute-done.2.refs_0_.refs_6_.refs_1_), channel_id=1, source_target_pairs={{3,2},{2,3},{7,6},{6,7},{11,10},{10,11},{15,14},{14,15},{19,18},{1... | collective-permute-start | bytes 1572872 | tf_op jit(solution)/shard_map/ppermute | solution.py:427
  15.0 0.1 collective-permute-start.3
  15.1 0.6 %collective-permute-done.1.source_ref.refs_1_.refs_2_.refs_3_.refs_0_.refs_7_ = f32[1032,128]{1,0:T(8,128)S(1)} collective-permute-done((f32[1032,128]{1,0:T(8,128)S(1)}, f32[1032,128]{1,0:T(8,128)S(1)}, u32[]{:S(2)}, u32[]{:S(2)}) %collective-permute-start.1) | collective-permute-done | bytes 528416 | tf_op jit(solution)/shard_map/ppermute | solution.py:427
  15.6 0.1 shard_map.40
  15.7 3.4 %collective-permute-start.4 = (f32[1032,128]{1,0:T(8,128)S(1)}, f32[1032,128]{1,0:T(8,128)S(1)}, u32[]{:S(2)}, u32[]{:S(2)}) collective-permute-start(f32[1032,128]{1,0:T(8,128)S(1)} %shard_map.40), channel_id=1, source_target_pairs={{2,0},{3,1},{0,2},{1,3},{6,4},{7,5},{4,6},{5,7},{10,8},{11,9},{8,1... | collective-permute-start | bytes 1585160 | tf_op jit(solution)/shard_map/ppermute | solution.py:427
  19.1 0.0 collective-permute-done.5.refs_2_.refs_8_
  19.1 0.1 shard_map.41.refs_0_
  19.2 1.6 %collective-permute-start.6 = (f32[1032,128]{1,0:T(8,128)S(1)}, f32[1032,128]{1,0:T(8,128)S(1)}, u32[]{:S(2)}, u32[]{:S(2)}) collective-permute-start(f32[1032,128]{1,0:T(8,128)S(1)} %shard_map.41.refs_0_), channel_id=1, source_target_pairs={{1,0},{0,1},{6,2},{7,3},{5,4},{4,5},{10,6},{11,7},{9,8},{8,9},{14,... | collective-permute-start | bytes 1585160 | tf_op jit(solution)/shard_map/ppermute | solution.py:427
  20.8 2.1 %shard_map.44.refs_11_.refs_4_ = f32[4,2,128,128]{3,2,1,0:T(8,128)S(1)} custom-call(s32[8,9]{1,0:T(8,128)S(1)} %shard_map.37.refs_4_.refs_0_, f32[4,4]{1,0:T(4,128)S(1)} %convert_element_type.9.refs_2_.refs_1_, f32[4,4]{1,0:T(4,128)S(1)} %convert_element_type.8.refs_0_.refs_2_, f32[4,4]{1,0:T(4,128)S(1)} %collective-permute-done.refs_1_.refs_3_.refs_2_, ...), custom_call_target="tpu_custom_call" | custom-call | tf_op jit(solution)/shard_map/pallas_call | solution.py:282
  22.9 0.0 collective-permute-done.7.refs_9_.refs_0_.refs_2_
  22.9 0.1 shard_map.49
  23.0 1.3 %collective-permute-start.8 = (f32[1032,128]{1,0:T(8,128)S(1)}, f32[1032,128]{1,0:T(8,128)S(1)}, u32[]{:S(2)}, u32[]{:S(2)}) collective-permute-start(f32[1032,128]{1,0:T(8,128)S(1)} %shard_map.49), channel_id=1, source_target_pairs={{2,0},{3,1},{6,4},{7,5},{10,8},{11,9},{14,12},{15,13},{18,16},{19,... | collective-permute-start | bytes 1585160 | tf_op jit(solution)/shard_map/ppermute | solution.py:427
  24.4 0.1 shard_map.48.refs_2_
  24.5 1.9 %collective-permute-done.3.refs_0_.refs_10_.refs_5_ = f32[1024,128]{1,0:T(8,128)S(1)} collective-permute-done((f32[1024,128]{1,0:T(8,128)S(1)}, f32[1024,128]{1,0:T(8,128)S(1)}, u32[]{:S(2)}, u32[]{:S(2)}) %collective-permute-start.3) | collective-permute-done | bytes 524320 | tf_op jit(solution)/shard_map/ppermute | solution.py:427
  26.4 0.0 collective-permute-done.4.source_ref.refs_8_.refs_3_
  26.4 1.8 %shard_map.45.refs_1_ = f32[4,2,128,128]{3,2,1,0:T(8,128)S(1)} custom-call(s32[8,9]{1,0:T(8,128)S(1)} %shard_map.37.refs_4_.refs_0_, f32[4,4]{1,0:T(4,128)S(1)} %convert_element_type.9.refs_2_.refs_1_, f32[4,4]{1,0:T(4,128)S(1)} %collective-permute-done.refs_1_.refs_3_.refs_2_, f32[8,128]{1,0:T(8,128)S(1)} %shard_map.42.refs_3_, ...), custom_call_target="tpu_custom_call" | custom-call | tf_op jit(solution)/shard_map/pallas_call | solution.py:282
  28.3 1.3 %collective-permute-done.6.source_ref.refs_3_ = f32[1032,128]{1,0:T(8,128)S(1)} collective-permute-done((f32[1032,128]{1,0:T(8,128)S(1)}, f32[1032,128]{1,0:T(8,128)S(1)}, u32[]{:S(2)}, u32[]{:S(2)}) %collective-permute-start.6) | collective-permute-done | bytes 528416 | tf_op jit(solution)/shard_map/ppermute | solution.py:427
  29.6 0.1 shard_map.47.refs_1_
  29.7 0.0 collective-permute-done.8.refs_4_
  29.7 1.8 %shard_map.50 = f32[8,128,128]{2,1,0:T(8,128)} custom-call(s32[8,9]{1,0:T(8,128)S(1)} %shard_map.37.refs_4_.refs_0_, f32[4,36]{1,0:T(4,128)S(1)} %shard_map.47.refs_1_, f32[2048,128]{1,0:T(8,128)S(1)} %shard_map.48.refs_2_, f32[1032,128]{1,0:T(8,128)S(1)} %collective-permute-done.6.source_ref.refs_3_, f32[1032,128]{1,0:T(8,128)S(1)} %collective-permute-done.8.refs_4_, ...), custom_call_target="tpu_custom_call" | custom-call | tf_op jit(solution)/shard_map/pallas_call | solution.py:395
  (5 shorter events, 0.1 us)
Async XLA Ops:
  0.0 3.7 %copy-start.2 = (s32[4,4]{1,0:T(4,128)S(1)}, s32[4,4]{1,0:T(4,128)}, u32[]{:S(2)}) copy-start(s32[4,4]{1,0:T(4,128)} %p_cols_ref.1) | copy-start | bytes 196
  0.0 11.9 %collective-permute-start.2 = (f32[1024,128]{1,0:T(8,128)}, f32[1024,128]{1,0:T(8,128)S(1)}, u32[]{:S(2)}, u32[]{:S(2)}) collective-permute-start(f32[1024,128]{1,0:T(8,128)} %bitcast.4), channel_id=1, source_target_pairs={{1,0},{0,1},{30,2},{31,3},{5,4},{4,5},{2,6},{3,7},{9,8},{8,9},{6,1... | collective-permute-start | bytes 1572872 | tf_op jit(solution)/shard_map/ppermute | solution.py:427
  2.8 2.4 %copy-start.3 = (s32[4,4]{1,0:T(4,128)S(1)}, s32[4,4]{1,0:T(4,128)}, u32[]{:S(2)}) copy-start(s32[4,4]{1,0:T(4,128)} %param.5) | copy-start | bytes 196
  2.8 2.4 %collective-permute-start = (f32[4,4]{1,0:T(4,128)S(1)}, f32[4,4]{1,0:T(4,128)S(1)}, u32[]{:S(2)}, u32[]{:S(2)}) collective-permute-start(f32[4,4]{1,0:T(4,128)S(1)} %convert_element_type.8.refs_0_.refs_2_), channel_id=1, source_target_pairs={{2,0},{3,1},{0,2},{1,3},{6,4},{7,5},{4,6},{5,7},{10,8},{11,9},{8,1... | collective-permute-start | bytes 200 | tf_op jit(solution)/shard_map/ppermute | solution.py:427
  5.2 1.0 %copy-start = (f32[4,2,128,128]{3,2,1,0:T(8,128)S(1)}, f32[4,2,128,128]{3,2,1,0:T(8,128)}, u32[]{:S(2)}) copy-start(f32[4,2,128,128]{3,2,1,0:T(8,128)} %param.3) | copy-start | bytes 1572868
  6.3 1.1 %copy-start.1 = (f32[4,2,128,128]{3,2,1,0:T(8,128)S(1)}, f32[4,2,128,128]{3,2,1,0:T(8,128)}, u32[]{:S(2)}) copy-start(f32[4,2,128,128]{3,2,1,0:T(8,128)} %param.3) | copy-start | bytes 1572868
  7.0 8.6 %collective-permute-start.1 = (f32[1032,128]{1,0:T(8,128)S(1)}, f32[1032,128]{1,0:T(8,128)S(1)}, u32[]{:S(2)}, u32[]{:S(2)}) collective-permute-start(f32[1032,128]{1,0:T(8,128)S(1)} %shard_map.38.refs_3_.refs_5_.refs_0_.refs_1_.refs_2_), channel_id=1, source_target_pairs={{28,0},{29,1},{3,2},{2,3},{0,4},{1,5},{7,6},{6,7},{4,8},{5,9},{11,... | collective-permute-start | bytes 1585160 | tf_op jit(solution)/shard_map/ppermute | solution.py:427
  7.3 11.8 %collective-permute-start.5 = (f32[1024,128]{1,0:T(8,128)S(1)}, f32[1024,128]{1,0:T(8,128)S(1)}, u32[]{:S(2)}, u32[]{:S(2)}) collective-permute-start(f32[1024,128]{1,0:T(8,128)S(1)} %bitcast.6), channel_id=1, source_target_pairs={{2,0},{3,1},{0,2},{1,3},{6,4},{7,5},{4,6},{5,7},{10,8},{11,9},{8,1... | collective-permute-start | bytes 1572872 | tf_op jit(solution)/shard_map/ppermute | solution.py:427
  11.9 11.0 %collective-permute-start.7 = (f32[1024,128]{1,0:T(8,128)S(1)}, f32[1024,128]{1,0:T(8,128)S(1)}, u32[]{:S(2)}, u32[]{:S(2)}) collective-permute-start(f32[1024,128]{1,0:T(8,128)S(1)} %collective-permute-done.2.refs_0_.refs_6_.refs_1_), channel_id=1, source_target_pairs={{3,2},{2,3},{7,6},{6,7},{11,10},{10,11},{15,14},{14,15},{19,18},{1... | collective-permute-start | bytes 1572872 | tf_op jit(solution)/shard_map/ppermute | solution.py:427
  15.0 11.4 %collective-permute-start.3 = (f32[1024,128]{1,0:T(8,128)S(1)}, f32[1024,128]{1,0:T(8,128)S(1)}, u32[]{:S(2)}, u32[]{:S(2)}) collective-permute-start(f32[1024,128]{1,0:T(8,128)S(1)} %collective-permute-done.2.refs_0_.refs_6_.refs_1_), channel_id=1, source_target_pairs={{2,0},{3,1},{4,2},{5,3},{6,4},{7,5},{8,6},{9,7},{10,8},{11,9},{12,... | collective-permute-start | bytes 1572872 | tf_op jit(solution)/shard_map/ppermute | solution.py:427
  15.7 10.7 %collective-permute-start.4 = (f32[1032,128]{1,0:T(8,128)S(1)}, f32[1032,128]{1,0:T(8,128)S(1)}, u32[]{:S(2)}, u32[]{:S(2)}) collective-permute-start(f32[1032,128]{1,0:T(8,128)S(1)} %shard_map.40), channel_id=1, source_target_pairs={{2,0},{3,1},{0,2},{1,3},{6,4},{7,5},{4,6},{5,7},{10,8},{11,9},{8,1... | collective-permute-start | bytes 1585160 | tf_op jit(solution)/shard_map/ppermute | solution.py:427
  19.2 10.4 %collective-permute-start.6 = (f32[1032,128]{1,0:T(8,128)S(1)}, f32[1032,128]{1,0:T(8,128)S(1)}, u32[]{:S(2)}, u32[]{:S(2)}) collective-permute-start(f32[1032,128]{1,0:T(8,128)S(1)} %shard_map.41.refs_0_), channel_id=1, source_target_pairs={{1,0},{0,1},{6,2},{7,3},{5,4},{4,5},{10,6},{11,7},{9,8},{8,9},{14,... | collective-permute-start | bytes 1585160 | tf_op jit(solution)/shard_map/ppermute | solution.py:427
  23.0 6.7 %collective-permute-start.8 = (f32[1032,128]{1,0:T(8,128)S(1)}, f32[1032,128]{1,0:T(8,128)S(1)}, u32[]{:S(2)}, u32[]{:S(2)}) collective-permute-start(f32[1032,128]{1,0:T(8,128)S(1)} %shard_map.49), channel_id=1, source_target_pairs={{2,0},{3,1},{6,4},{7,5},{10,8},{11,9},{14,12},{15,13},{18,16},{19,... | collective-permute-start | bytes 1585160 | tf_op jit(solution)/shard_map/ppermute | solution.py:427
